TPU v7x, 256 devices: a whole 4x4x8 slice. The times are simulated.
256 devices in a mesh: dp: 32 (over x, y, core), section: 8 (over z).
Axes of the slice: x: 4, y: 4, z: 8, core: 2. Of those that a mesh axis runs over, the one named last changes fastest.
Arguments:
- hidden_in: bfloat16 [8, 4096, 8192], P('section', 'dp'), may hold values from -6 to 6
- weight_rows: bfloat16 [8, 8192, 768], P('section', 'dp'), may hold values from -0.0625 to 0.0625
- x_in: bfloat16 [8, 4096, 12288], P('section', 'dp'), may hold values from -6 to 6
- c_in: bfloat16 [8, 4096, 768], P('section', 'dp'), may hold values from -0.59765625 to 0.59765625
- step_size: float32 [8, 4096, 192], P('section', 'dp'), may hold values from 0 to 1, as said below
- a_log: float32 [8, 192], P('section'), may hold values from 0.7 to 1.8
- out_grad: bfloat16 [8, 4096, 12288], P('section', 'dp'), may hold values from -6 to 6
Outputs:
- weight_grads: bfloat16 [8, 8192, 768], P('section', 'dp')
- next_cotangent: bfloat16 [8, 4096, 8192], P('section', 'dp')
- step_size_gradients: float32 [8, 4096, 192], P('section', 'dp')
Inputs may be any that keep to these rules, and one draw needn't show every extreme that they name: `step_size`: positive step sizes.
All inputs are finite; a program needn't handle non-finite values.
Results may differ from a plain program's by a relative error of at most 0.025.
Values may be sent and summed in bfloat16 or wider, within the bound.
No kernel may reach another device: no remote copies, remote signals or barrier semaphores. Data moves between devices by JAX's collectives and lax.ppermute only.
A program may use at most 128 MiB of HBM per device.

v0:
```python
import functools

import jax
import jax.numpy as jnp
import numpy as np
from jax import lax
from jax.experimental import pallas as pl
from jax.experimental.pallas import tpu as pltpu
from jax.sharding import Mesh
from jax.sharding import PartitionSpec as P

STATE = 128
TOK = 128
HEADS = 192
GROUPS = 6
PER_GROUP = HEADS // GROUPS
HEAD_DIM = 64
RING = 4
SHARD = 256
OFFSETS = (0, 3, 1, 2)
LOG2E = float(np.log2(np.e))
FAR_BELOW = -1e30
HP = lax.Precision.HIGHEST
F32 = jnp.float32
BF16 = jnp.bfloat16


def ring_shift(shard, first, by):
    pairs = []
    for x in range(RING):
        for y in range(RING):
            for core in range(2):
                if first == (core == 0):
                    target = ((x + by) % RING, y)
                else:
                    target = (x, (y + by) % RING)
                pairs.append(((x * RING + y) * 2 + core, (target[0] * RING + target[1]) * 2 + core))
    return lax.ppermute(shard, ("x", "y", "core"), pairs)


def swap_cores(shard):
    return lax.ppermute(shard, "core", [(0, 1), (1, 0)])


def to_previous_section(shard):
    return lax.ppermute(shard, "section", [(s, s - 1) for s in range(1, lax.axis_size("section"))])


def coordinates():
    return jnp.stack([lax.axis_index(a) for a in ("x", "y", "core")]).astype(jnp.int32)


def block_columns(where_ref, k, crossed):
    core = 1 - where_ref[2] if crossed else where_ref[2]
    first, second = OFFSETS[k % RING], OFFSETS[k // RING]
    dx = first + core * (second - first)
    dy = second + core * (first - second)
    chip = ((where_ref[0] + dx) & (RING - 1)) * RING + ((where_ref[1] + dy) & (RING - 1))
    return pl.multiple_of((chip * 2 + core) * SHARD, SHARD)


BLOCKS = RING * RING
VMEM_LIMIT = 16 * 2**20
SMALL_COST = pl.CostEstimate(flops=0, bytes_accessed=1024, transcendentals=0)


def split_columns_kernel(where_ref, hidden_ref, keep_ref, send_ref):
    for k in range(BLOCKS):
        to = slice(k * SHARD, (k + 1) * SHARD)
        keep_ref[:, to] = hidden_ref[:, pl.ds(block_columns(where_ref, k, False), SHARD)]
        send_ref[:, to] = hidden_ref[:, pl.ds(block_columns(where_ref, k, True), SHARD)]


def split_columns(where, hidden):
    halved = jax.ShapeDtypeStruct((TOK, hidden.shape[1] // 2), hidden.dtype)
    in_vmem = pl.BlockSpec(memory_space=pltpu.VMEM)
    return pl.pallas_call(
        split_columns_kernel,
        in_specs=[pl.BlockSpec(memory_space=pltpu.SMEM), in_vmem],
        out_specs=[in_vmem, in_vmem],
        out_shape=[halved, halved],
        cost_estimate=SMALL_COST,
        compiler_params=pltpu.CompilerParams(vmem_limit_bytes=VMEM_LIMIT),
        name="split_columns",
    )(where, hidden)


def join_columns_kernel(orders, where_ref, *refs):
    pieces, out_ref = refs[:-1], refs[-1]
    for i, order in enumerate(orders):
        for side in range(2):
            for j, k in enumerate(order):
                columns = pl.ds(block_columns(where_ref, k, side == 1), SHARD)
                out_ref[:, columns] = pieces[2 * i + side][:TOK, j * SHARD : (j + 1) * SHARD]


def join_columns(where, pieces, orders, width):
    return pl.pallas_call(
        functools.partial(join_columns_kernel, orders),
        in_specs=[pl.BlockSpec(memory_space=pltpu.SMEM)]
        + [pl.BlockSpec(memory_space=pltpu.VMEM)] * len(pieces),
        out_specs=pl.BlockSpec(memory_space=pltpu.VMEM),
        out_shape=jax.ShapeDtypeStruct((TOK, width), BF16),
        cost_estimate=SMALL_COST,
        compiler_params=pltpu.CompilerParams(vmem_limit_bytes=VMEM_LIMIT),
        name="join_columns",
    )(where, *pieces)


def iotas():
    rows = lax.broadcasted_iota(jnp.int32, (TOK, TOK), 0)
    lanes = lax.broadcasted_iota(jnp.int32, (TOK, TOK), 1)
    return rows, lanes


def prepare(step_ref, alog_ref, rate_t, parts, left, right):
    rows, lanes = iotas()

    @pl.when(pl.program_id(0) == 0)
    def _():
        rate_t[...] = jnp.broadcast_to(jnp.exp(alog_ref[...]), (TOK, HEADS)).T
        left[:, :TOK] = (rows == lanes).astype(F32).astype(BF16)
        mask = jnp.where(rows >= lanes, 0.0, FAR_BELOW).astype(BF16)
        for h in range(PER_GROUP):
            at = slice(h * TOK, (h + 1) * TOK)
            chosen = (rows < 3 * PER_GROUP) & (rows % PER_GROUP == h)
            right[:TOK, at] = mask
            right[TOK:, at] = jnp.where(chosen, 1.0, 0.0).astype(BF16)

    upper = (rows <= lanes).astype(F32)
    rates = rate_t[group_rows(), :]
    cumul = jnp.dot(
        step_ref[...] * (rates * -LOG2E), upper, precision=HP, preferred_element_type=F32
    )
    high = cumul.astype(BF16).astype(F32)
    middle = (cumul - high).astype(BF16).astype(F32)
    low = cumul - high - middle
    ones = jnp.where(lax.broadcasted_iota(jnp.int32, (PER_GROUP, TOK), 0) < 3, 1.0, 0.0)
    left[:, TOK:] = jnp.concatenate([high, middle, low, ones], axis=0).T.astype(BF16)
    for i, part in enumerate((high, middle, low)):
        parts[i * PER_GROUP : (i + 1) * PER_GROUP, :] = part
    place = lax.broadcasted_iota(jnp.int32, (16, TOK), 0)
    for h in range(PER_GROUP):
        rest = jnp.zeros((16, TOK), F32)
        for i in range(3):
            rest = jnp.where(place == i, -parts[i * PER_GROUP + h : i * PER_GROUP + h + 1, :], rest)
        right[TOK + 3 * PER_GROUP : TOK + 3 * PER_GROUP + 16, h * TOK : (h + 1) * TOK] = rest.astype(BF16)
    return rates


def head_products(x_ref, grad_ref, step_ref, left, right):
    lanes = lax.broadcasted_iota(jnp.int32, (TOK, 2 * HEAD_DIM), 1)
    first = lanes < HEAD_DIM
    zero = jnp.zeros((), BF16)
    for pair in range(PER_GROUP // 2):
        at = slice(pair * 2 * HEAD_DIM, (pair + 1) * 2 * HEAD_DIM)
        both = x_ref[:, at]
        apart = jnp.concatenate([jnp.where(first, both, zero), jnp.where(first, zero, both)], axis=0)
        products = lax.dot_general(
            grad_ref[:, at], apart, (((1,), (1,)), ((), ())), preferred_element_type=F32
        )
        differ = jnp.dot(
            left[...], right[:, 2 * pair * TOK : 2 * (pair + 1) * TOK], preferred_element_type=F32
        )
        products = jnp.exp2(differ) * products
        for k in range(2):
            h = 2 * pair + k
            yield h, products[:, k * TOK : (k + 1) * TOK], step_ref[h : h + 1, :]


def group_rows():
    return pl.ds(pl.multiple_of(pl.program_id(0) * PER_GROUP, PER_GROUP), PER_GROUP)


def sum_of_heads(x_ref, grad_ref, c_ref, step_ref, left, right, out_ref):
    total = jnp.zeros((TOK, TOK), F32)
    for _, product, steps in head_products(x_ref, grad_ref, step_ref, left, right):
        total = total + product * steps
    grad_b = lax.dot_general(
        total, c_ref[...].astype(F32), (((0,), (0,)), ((), ())),
        precision=HP, preferred_element_type=F32,
    )
    out_ref[...] = grad_b.astype(BF16)


def grad_b_kernel(
    x_ref, grad_ref, c_ref, step_ref, alog_ref, out_ref, rate_t, parts, left, right
):
    prepare(step_ref, alog_ref, rate_t, parts, left, right)
    sum_of_heads(x_ref, grad_ref, c_ref, step_ref, left, right, out_ref)


def step_grad_kernel(
    x_ref, grad_ref, c_ref, b_ref, step_ref, alog_ref, out_ref, rate_t, parts, left, right, direct
):
    rates = prepare(step_ref, alog_ref, rate_t, parts, left, right)
    rows, lanes = iotas()
    scores = lax.dot_general(
        c_ref[...], b_ref[...], (((1,), (1,)), ((), ())), preferred_element_type=F32
    )
    by_row = jnp.zeros((TOK, TOK), F32)
    for h, product, steps in head_products(x_ref, grad_ref, step_ref, left, right):
        weighted = product * scores
        direct[h : h + 1, :] = jnp.sum(weighted, axis=0, keepdims=True)
        by_row = jnp.where(lanes == h, jnp.sum(weighted * steps, axis=1, keepdims=True), by_row)
    cumul_grad = by_row.T[:PER_GROUP] - direct[...] * step_ref[...]
    lower = (rows >= lanes).astype(F32)
    later = jnp.dot(cumul_grad, lower, precision=HP, preferred_element_type=F32)
    out_ref[...] = direct[...] - rates * later


WIDE = PER_GROUP * HEAD_DIM
BY_GROUP = pl.BlockSpec((TOK, STATE), lambda g: (0, g))
BY_HEADS = pl.BlockSpec((TOK, WIDE), lambda g: (0, g))
STEP_ROWS = pl.BlockSpec((PER_GROUP, TOK), lambda g: (g, 0))
WHOLE_RATE = pl.BlockSpec((1, HEADS), lambda g: (0, 0))
SCAN_SCRATCH = [
    pltpu.VMEM((HEADS, TOK), F32),
    pltpu.VMEM((3 * PER_GROUP, TOK), F32),
    pltpu.VMEM((TOK, 2 * TOK), BF16),
    pltpu.VMEM((2 * TOK, PER_GROUP * TOK), BF16),
]


def scan_grad_b(x, grad, c, steps_t, a_log):
    return pl.pallas_call(
        grad_b_kernel,
        grid=(GROUPS,),
        in_specs=[BY_HEADS, BY_HEADS, BY_GROUP, STEP_ROWS, WHOLE_RATE],
        out_specs=BY_GROUP,
        out_shape=jax.ShapeDtypeStruct((TOK, GROUPS * STATE), BF16),
        scratch_shapes=SCAN_SCRATCH,
        cost_estimate=SMALL_COST,
        compiler_params=pltpu.CompilerParams(vmem_limit_bytes=56 * 2**20),
        name="scan_grad_b",
    )(x, grad, c, steps_t, a_log)


def scan_step_grad(x, grad, c, b, steps_t, a_log):
    return pl.pallas_call(
        step_grad_kernel,
        grid=(GROUPS,),
        in_specs=[BY_HEADS, BY_HEADS, BY_GROUP, BY_GROUP, STEP_ROWS, WHOLE_RATE],
        out_specs=STEP_ROWS,
        out_shape=jax.ShapeDtypeStruct((HEADS, TOK), F32),
        scratch_shapes=SCAN_SCRATCH + [pltpu.VMEM((PER_GROUP, TOK), F32)],
        cost_estimate=SMALL_COST,
        compiler_params=pltpu.CompilerParams(vmem_limit_bytes=VMEM_LIMIT),
        name="scan_step_grad",
    )(x, grad, c, b, steps_t, a_log)


def rows_dot(a, b):
    return jnp.dot(a, b, preferred_element_type=F32)


def outer_dot(a, b):
    return lax.dot_general(a, b, (((0,), (0,)), ((), ())), preferred_element_type=F32)


def against_rows(a, w):
    return lax.dot_general(a, w, (((1,), (1,)), ((), ())), preferred_element_type=F32).astype(BF16)


def after(values, *done):
    return lax.optimization_barrier((values, done))[0]


def body(hidden_in, weight_rows, x_in, c_in, step_size, a_log, out_grad):
    hidden, part = hidden_in[0], weight_rows[0]
    x, c, steps_t, grad = x_in[0], c_in[0], step_size[0].T, out_grad[0]
    where = coordinates()
    block = RING * SHARD

    near = [ring_shift(part, True, by) for by in (1, -1, 2)]
    grad_b = scan_grad_b(x, grad, c, steps_t, a_log)
    near = jnp.concatenate([part] + after(near, grad_b))
    far = [ring_shift(near, False, by) for by in (1, -1)]
    both_b = jnp.concatenate([grad_b, swap_cores(grad_b)])

    def pass_on(rows, *done):
        both = after(to_previous_section(against_rows(both_b, rows)), *done)
        return both, swap_cores(both[TOK:])

    passed = [pass_on(near, far)]
    kept, sent = split_columns(after(where, both_b), hidden)
    both_hidden = jnp.concatenate([kept, swap_cores(sent)])

    half = block // 2
    last = jnp.concatenate([ring_shift(far[0][:half], False, 1), ring_shift(far[1][half:], False, -1)])

    def columns(i):
        return both_hidden[:, i * block : (i + 1) * block]

    def payload(i):
        return jnp.concatenate([columns(i), both_b], axis=1)

    sends = after([payload(1), payload(2)], far)
    arrived = [ring_shift(p, False, by) for p, by in zip(sends, (-1, 1))]
    arrived.append(ring_shift(after(payload(3), last, passed[0], arrived[0]), False, 2))

    proj = jnp.zeros((2 * TOK, GROUPS * STATE), F32)
    for i, rows in enumerate((near, *far, last)):
        proj += rows_dot(columns(i), rows)
    proj_b = (proj[:TOK] + swap_cores(proj[TOK:])).astype(BF16)
    step_grads_t = scan_step_grad(x, grad, c, proj_b, steps_t, a_log)

    arrived = [after(p, step_grads_t) for p in arrived]
    passed.append(pass_on(jnp.concatenate(far), step_grads_t))
    passed.append(pass_on(after(last, passed[1][0])))
    sums = outer_dot(columns(0), both_b)
    for p in arrived:
        sums += outer_dot(p[:, :block], p[:, block:])
    parts = after(sums.astype(BF16), passed[0], passed[1])
    shifts = ((1, -1), (2, 1), (3, 2))
    others = [ring_shift(parts[i * SHARD : (i + 1) * SHARD], True, by) for i, by in shifts]

    orders = (tuple(range(RING)), tuple(range(RING, 3 * RING)), tuple(range(3 * RING, 4 * RING)))
    joined = join_columns(where, passed[0] + passed[1] + passed[2], orders, hidden.shape[1])
    weight_grads = sums[:SHARD]
    for other in after(others, joined):
        weight_grads += other.astype(F32)
    return weight_grads.astype(BF16)[None], joined[None], step_grads_t.T[None]


def solution(mesh):
    fine = Mesh(
        mesh.devices.reshape(RING, RING, 2, mesh.shape["section"]), ("x", "y", "core", "section")
    )
    dp = ("x", "y", "core")
    split = P("section", dp, None)
    in_specs = (split, split, split, split, split, P("section", None), split)
    return jax.shard_map(
        body, mesh=fine, in_specs=in_specs, out_specs=(split, split, split), check_vma=False
    )
```

profile of v0, /device:TPU:1, one launch (start us, length us, event | category | flops | bytes accessed | tf_op | source)
XLA Modules:
  0.0 98.3 jit_solution(12724833729144744593)
XLA Ops:
  0.6 3.8 %collective-permute-start.4 = (bf16[256,768]{1,0:T(8,128)(2,1)}, bf16[256,768]{1,0:T(8,128)(2,1)S(1)}, u32[]{:S(2)}, u32[]{:S(2)}) collective-permute-start(bf16[256,768]{1,0:T(8,128)(2,1)} %bitcast.33), channel_id=1, source_target_pairs={{0,128},{8,40},{16,144},{24,56},{32,160},{40,8},{48,176},{56,24},{... | collective-permute-start | bytes 1179656 | tf_op jit(solution)/shard_map/ppermute | solution.py:38
  4.5 0.8 collective-permute-start.3
  5.2 0.7 collective-permute-start.2
  6.0 1.6 %copy-done.2 = bf16[1,128,8192]{2,1,0:T(8,128)(2,1)S(1)} copy-done((bf16[1,128,8192]{2,1,0:T(8,128)(2,1)S(1)}, bf16[1,128,8192]{2,1,0:T(8,128)(2,1)}, u32[]{:S(2)}) %copy-start.2) | copy-done | bytes 2097176
  7.6 0.8 split_columns.1
  8.4 1.4 %collective-permute-start.1 = (bf16[128,4096]{1,0:T(8,128)(2,1)S(1)}, bf16[128,4096]{1,0:T(8,128)(2,1)S(1)}, u32[]{:S(2)}, u32[]{:S(2)}) collective-permute-start(bf16[128,4096]{1,0:T(8,128)(2,1)S(1)} %get-tuple-element.24), channel_id=1, source_target_pairs={{0,8},{8,0},{1,9},{9,1},{2,10},{10,2},{3,11},{11,3},{4,12},{12,4},... | collective-permute-start | bytes 3145736 | tf_op jit(solution)/shard_map/ppermute | solution.py:42
  9.9 10.0 %scan_grad_b.1 = bf16[128,768]{1,0:T(8,128)(2,1)} custom-call(bf16[128,12288]{1,0:T(8,128)(2,1)} %bitcast.23, bf16[128,12288]{1,0:T(8,128)(2,1)} %bitcast.25, bf16[128,768]{1,0:T(8,128)(2,1)} %bitcast.28, f32[192,128]{1,0:T(8,128)} %bitcast.30, f32[1,192]{1,0:T(1,128)} %alog_ref.3), custom_call_target="tpu_custom_call" | custom-call | bytes 1024 | tf_op jit(solution)/shard_map/scan_grad_b/pallas_call | solution.py:226
  20.0 2.1 %collective-permute-start.6 = (bf16[1024,768]{1,0:T(8,128)(2,1)S(1)}, bf16[1024,768]{1,0:T(8,128)(2,1)S(1)}, u32[]{:S(2)}, u32[]{:S(2)}) collective-permute-start(bf16[1024,768]{1,0:T(8,128)(2,1)S(1)} %pad_maximum_fusion), channel_id=1, source_target_pairs={{0,48},{8,200},{16,0},{24,216},{32,16},{40,232},{48,32},{56,248},{... | collective-permute-start | bytes 4718600 | tf_op jit(solution)/shard_map/ppermute | solution.py:38
  22.9 1.3 %collective-permute-start.12 = (bf16[256,1024]{1,0:T(8,128)(2,1)S(1)}, bf16[256,1024]{1,0:T(8,128)(2,1)S(1)}, u32[]{:S(2)}, u32[]{:S(2)}) collective-permute-start(bf16[256,1024]{1,0:T(8,128)(2,1)S(1)} %convolution_convert_fusion.1), channel_id=1, source_target_pairs={{1,0},{2,1},{3,2},{4,3},{5,4},{6,5},{7,6},{9,8},{10,9},{11,10},{12... | collective-permute-start | bytes 1572872 | tf_op jit(solution)/shard_map/ppermute | solution.py:46
  24.6 15.0 %collective-permute-done.6 = bf16[1024,768]{1,0:T(8,128)(2,1)S(1)} collective-permute-done((bf16[1024,768]{1,0:T(8,128)(2,1)S(1)}, bf16[1024,768]{1,0:T(8,128)(2,1)S(1)}, u32[]{:S(2)}, u32[]{:S(2)}) %collective-permute-start.6) | collective-permute-done | bytes 1572896 | tf_op jit(solution)/shard_map/ppermute | solution.py:38
  39.7 3.4 %collective-permute-start.9 = (bf16[512,768]{1,0:T(8,128)(2,1)S(1)}, bf16[512,768]{1,0:T(8,128)(2,1)S(1)}, u32[]{:S(2)}, u32[]{:S(2)}) collective-permute-start(bf16[512,768]{1,0:T(8,128)(2,1)S(1)} %slice.93), channel_id=1, source_target_pairs={{0,48},{8,200},{16,0},{24,216},{32,16},{40,232},{48,32},{56,248},{... | collective-permute-start | bytes 2359304 | tf_op jit(solution)/shard_map/ppermute | solution.py:38
  43.2 1.0 %fusion.4 = bf16[256,2048]{1,0:T(8,128)(2,1)S(1)} fusion(bf16[1024,768]{1,0:T(8,128)(2,1)S(1)} %collective-permute-done.6, bf16[1024,768]{1,0:T(8,128)(2,1)S(1)} %collective-permute-done.5, bf16[128,768]{1,0:T(8,128)(2,1)S(1)} %collective-permute-done, bf16[128,768]{1,0:T(8,128)(2,1)S(1)} %copy-done.6), kind=kOutput, calls=%fused_computation.5 | convolution fusion | flops 812908544 | bytes 4587520 | tf_op jit(solution)/shard_map/dot_general | solution.py:262
  44.3 1.3 %collective-permute-start.15 = (bf16[256,2048]{1,0:T(8,128)(2,1)S(1)}, bf16[256,2048]{1,0:T(8,128)(2,1)S(1)}, u32[]{:S(2)}, u32[]{:S(2)}) collective-permute-start(bf16[256,2048]{1,0:T(8,128)(2,1)S(1)} %fusion.4), channel_id=1, source_target_pairs={{1,0},{2,1},{3,2},{4,3},{5,4},{6,5},{7,6},{9,8},{10,9},{11,10},{12... | collective-permute-start | bytes 3145736 | tf_op jit(solution)/shard_map/ppermute | solution.py:46
  45.6 2.9 %collective-permute-start.7 = (bf16[256,1792]{1,0:T(8,128)(2,1)S(1)}, bf16[256,1792]{1,0:T(8,128)(2,1)S(1)}, u32[]{:S(2)}, u32[]{:S(2)}) collective-permute-start(bf16[256,1792]{1,0:T(8,128)(2,1)S(1)} %get-tuple-element.28), channel_id=1, source_target_pairs={{0,48},{8,200},{16,0},{24,216},{32,16},{40,232},{48,32},{56,248},{... | collective-permute-start | bytes 2752520 | tf_op jit(solution)/shard_map/ppermute | solution.py:38
  49.6 5.9 %collective-permute-done.8 = bf16[512,768]{1,0:T(8,128)(2,1)S(1)} collective-permute-done((bf16[512,768]{1,0:T(8,128)(2,1)S(1)}, bf16[512,768]{1,0:T(8,128)(2,1)S(1)}, u32[]{:S(2)}, u32[]{:S(2)}) %collective-permute-start.8) | collective-permute-done | bytes 786464 | tf_op jit(solution)/shard_map/ppermute | solution.py:38
  57.0 3.2 %collective-permute-start.10 = (f32[128,768]{1,0:T(8,128)S(1)}, f32[128,768]{1,0:T(8,128)S(1)}, u32[]{:S(2)}, u32[]{:S(2)}) collective-permute-start(f32[128,768]{1,0:T(8,128)S(1)} %slice.95), channel_id=1, source_target_pairs={{0,8},{8,0},{1,9},{9,1},{2,10},{10,2},{3,11},{11,3},{4,12},{12,4},... | collective-permute-start | bytes 1179656 | tf_op jit(solution)/shard_map/ppermute | solution.py:42
  60.7 0.6 fusion.18
  61.3 0.9 collective-permute-done.13.refs_1_
  62.2 2.9 %collective-permute-start.14 = (bf16[256,1792]{1,0:T(8,128)(2,1)S(1)}, bf16[256,1792]{1,0:T(8,128)(2,1)S(1)}, u32[]{:S(2)}, u32[]{:S(2)}) collective-permute-start(bf16[256,1792]{1,0:T(8,128)(2,1)S(1)} %get-tuple-element.33), channel_id=1, source_target_pairs={{0,32},{8,136},{16,48},{24,152},{32,0},{40,168},{48,16},{56,184},{... | collective-permute-start | bytes 2752520 | tf_op jit(solution)/shard_map/ppermute | solution.py:38
  65.2 9.8 %scan_step_grad.1 = f32[192,128]{1,0:T(8,128)} custom-call(bf16[128,12288]{1,0:T(8,128)(2,1)S(1)} %bitcast.24, bf16[128,12288]{1,0:T(8,128)(2,1)S(1)} %bitcast.26, bf16[128,768]{1,0:T(8,128)(2,1)S(1)} %bitcast.29, bf16[128,768]{1,0:T(8,128)(2,1)S(1)} %fusion.21.b_ref, f32[192,128]{1,0:T(8,128)S(1)} %bitcast.31, f32[1,192]{1,0:T(1,128)S(1)} %copy-done.5), custom_call_target="tpu_custom_call" | custom-call | bytes 1024 | tf_op jit(solution)/shard_map/scan_step_grad/pallas_call | solution.py:240
  75.1 1.6 %collective-permute-start.16 = (bf16[128,2048]{1,0:T(8,128)(2,1)S(1)}, bf16[128,2048]{1,0:T(8,128)(2,1)S(1)}, u32[]{:S(2)}, u32[]{:S(2)}) collective-permute-start(bf16[128,2048]{1,0:T(8,128)(2,1)S(1)} %slice.83), channel_id=1, source_target_pairs={{0,8},{8,0},{1,9},{9,1},{2,10},{10,2},{3,11},{11,3},{4,12},{12,4},... | collective-permute-start | bytes 1572872 | tf_op jit(solution)/shard_map/ppermute | solution.py:42
  77.3 1.3 %collective-permute-start.20 = (bf16[256,1024]{1,0:T(8,128)(2,1)S(1)}, bf16[256,1024]{1,0:T(8,128)(2,1)S(1)}, u32[]{:S(2)}, u32[]{:S(2)}) collective-permute-start(bf16[256,1024]{1,0:T(8,128)(2,1)S(1)} %convolution_convert_fusion), channel_id=1, source_target_pairs={{1,0},{2,1},{3,2},{4,3},{5,4},{6,5},{7,6},{9,8},{10,9},{11,10},{12... | collective-permute-start | bytes 1572872 | tf_op jit(solution)/shard_map/ppermute | solution.py:46
  78.6 0.6 fusion.13
  79.2 0.6 fusion.15
  79.9 4.2 %collective-permute-done.14 = bf16[256,1792]{1,0:T(8,128)(2,1)S(1)} collective-permute-done((bf16[256,1792]{1,0:T(8,128)(2,1)S(1)}, bf16[256,1792]{1,0:T(8,128)(2,1)S(1)}, u32[]{:S(2)}, u32[]{:S(2)}) %collective-permute-start.14) | collective-permute-done | bytes 917536 | tf_op jit(solution)/shard_map/ppermute | solution.py:38
  84.1 0.7 fusion.34
  85.1 2.7 %collective-permute-start.17 = (bf16[256,768]{1,0:T(8,128)(2,1)S(1)}, bf16[256,768]{1,0:T(8,128)(2,1)S(1)}, u32[]{:S(2)}, u32[]{:S(2)}) collective-permute-start(bf16[256,768]{1,0:T(8,128)(2,1)S(1)} %get-tuple-element.46), channel_id=1, source_target_pairs={{0,192},{8,56},{16,208},{24,8},{32,224},{40,24},{48,240},{56,40},{... | collective-permute-start | bytes 1179656 | tf_op jit(solution)/shard_map/ppermute | solution.py:38
  87.7 5.3 %collective-permute-done.20.refs_4_ = bf16[256,1024]{1,0:T(8,128)(2,1)S(1)} collective-permute-done((bf16[256,1024]{1,0:T(8,128)(2,1)S(1)}, bf16[256,1024]{1,0:T(8,128)(2,1)S(1)}, u32[]{:S(2)}, u32[]{:S(2)}) %collective-permute-start.20) | collective-permute-done | bytes 524320 | tf_op jit(solution)/shard_map/ppermute | solution.py:46
  93.0 0.8 collective-permute-start.21
  93.8 1.2 %collective-permute-done.21.refs_5_ = bf16[128,1024]{1,0:T(8,128)(2,1)S(1)} collective-permute-done((bf16[128,1024]{1,0:T(8,128)(2,1)S(1)}, bf16[128,1024]{1,0:T(8,128)(2,1)S(1)}, u32[]{:S(2)}, u32[]{:S(2)}) %collective-permute-start.21) | collective-permute-done | bytes 262176 | tf_op jit(solution)/shard_map/ppermute | solution.py:42
  95.0 2.1 %join_columns.1 = bf16[128,8192]{1,0:T(8,128)(2,1)} custom-call(s32[3]{0:T(128)S(1)} %pad_add_fusion.where_ref, bf16[256,1024]{1,0:T(8,128)(2,1)S(1)} %collective-permute-done.12.refs_0_, bf16[128,1024]{1,0:T(8,128)(2,1)S(1)} %collective-permute-done.13.refs_1_, bf16[256,2048]{1,0:T(8,128)(2,1)S(1)} %collective-permute-done.15.refs_2_, ...), custom_call_target="tpu_custom_call" | custom-call | bytes 1024 | tf_op jit(solution)/shard_map/join_columns/pallas_call | solution.py:98
  97.4 0.9 fusion.20
  (60 shorter events, 5.7 us)
Async XLA Ops:
  0.6 19.3 %collective-permute-start.4 = (bf16[256,768]{1,0:T(8,128)(2,1)}, bf16[256,768]{1,0:T(8,128)(2,1)S(1)}, u32[]{:S(2)}, u32[]{:S(2)}) collective-permute-start(bf16[256,768]{1,0:T(8,128)(2,1)} %bitcast.33), channel_id=1, source_target_pairs={{0,128},{8,40},{16,144},{24,56},{32,160},{40,8},{48,176},{56,24},{... | collective-permute-start | bytes 1179656 | tf_op jit(solution)/shard_map/ppermute | solution.py:38
  4.5 15.5 %collective-permute-start.3 = (bf16[256,768]{1,0:T(8,128)(2,1)}, bf16[256,768]{1,0:T(8,128)(2,1)S(1)}, u32[]{:S(2)}, u32[]{:S(2)}) collective-permute-start(bf16[256,768]{1,0:T(8,128)(2,1)} %bitcast.34), channel_id=1, source_target_pairs={{0,192},{8,56},{16,208},{24,8},{32,224},{40,24},{48,240},{56,40},{... | collective-permute-start | bytes 1179656 | tf_op jit(solution)/shard_map/ppermute | solution.py:38
  5.2 14.7 %collective-permute-start.2 = (bf16[256,768]{1,0:T(8,128)(2,1)}, bf16[256,768]{1,0:T(8,128)(2,1)S(1)}, u32[]{:S(2)}, u32[]{:S(2)}) collective-permute-start(bf16[256,768]{1,0:T(8,128)(2,1)} %bitcast.35), channel_id=1, source_target_pairs={{0,64},{8,24},{16,80},{24,40},{32,96},{40,56},{48,112},{56,8},{64,... | collective-permute-start | bytes 1179656 | tf_op jit(solution)/shard_map/ppermute | solution.py:38
  6.0 1.6 %copy-start.2 = (bf16[1,128,8192]{2,1,0:T(8,128)(2,1)S(1)}, bf16[1,128,8192]{2,1,0:T(8,128)(2,1)}, u32[]{:S(2)}) copy-start(bf16[1,128,8192]{2,1,0:T(8,128)(2,1)} %param.7) | copy-start | bytes 6291460
  8.4 15.8 %collective-permute-start.1 = (bf16[128,4096]{1,0:T(8,128)(2,1)S(1)}, bf16[128,4096]{1,0:T(8,128)(2,1)S(1)}, u32[]{:S(2)}, u32[]{:S(2)}) collective-permute-start(bf16[128,4096]{1,0:T(8,128)(2,1)S(1)} %get-tuple-element.24), channel_id=1, source_target_pairs={{0,8},{8,0},{1,9},{9,1},{2,10},{10,2},{3,11},{11,3},{4,12},{12,4},... | collective-permute-start | bytes 3145736 | tf_op jit(solution)/shard_map/ppermute | solution.py:42
  9.9 10.1 %copy-start.7 = (bf16[1,256,768]{2,1,0:T(8,128)(2,1)S(1)}, bf16[1,256,768]{2,1,0:T(8,128)(2,1)}, u32[]{:S(2)}) copy-start(bf16[1,256,768]{2,1,0:T(8,128)(2,1)} %param.8) | copy-start | bytes 1179652
  19.9 2.4 %copy-start.6 = (bf16[128,768]{1,0:T(8,128)(2,1)S(1)}, bf16[128,768]{1,0:T(8,128)(2,1)}, u32[]{:S(2)}) copy-start(bf16[128,768]{1,0:T(8,128)(2,1)} %scan_grad_b.1) | copy-start | bytes 589828
  19.9 2.4 %collective-permute-start = (bf16[128,768]{1,0:T(8,128)(2,1)}, bf16[128,768]{1,0:T(8,128)(2,1)S(1)}, u32[]{:S(2)}, u32[]{:S(2)}) collective-permute-start(bf16[128,768]{1,0:T(8,128)(2,1)} %scan_grad_b.1), channel_id=1, source_target_pairs={{0,8},{8,0},{1,9},{9,1},{2,10},{10,2},{3,11},{11,3},{4,12},{12,4},... | collective-permute-start | bytes 589832 | tf_op jit(solution)/shard_map/ppermute | solution.py:42
  20.0 19.6 %collective-permute-start.6 = (bf16[1024,768]{1,0:T(8,128)(2,1)S(1)}, bf16[1024,768]{1,0:T(8,128)(2,1)S(1)}, u32[]{:S(2)}, u32[]{:S(2)}) collective-permute-start(bf16[1024,768]{1,0:T(8,128)(2,1)S(1)} %pad_maximum_fusion), channel_id=1, source_target_pairs={{0,48},{8,200},{16,0},{24,216},{32,16},{40,232},{48,32},{56,248},{... | collective-permute-start | bytes 4718600 | tf_op jit(solution)/shard_map/ppermute | solution.py:38
  22.2 20.9 %collective-permute-start.5 = (bf16[1024,768]{1,0:T(8,128)(2,1)S(1)}, bf16[1024,768]{1,0:T(8,128)(2,1)S(1)}, u32[]{:S(2)}, u32[]{:S(2)}) collective-permute-start(bf16[1024,768]{1,0:T(8,128)(2,1)S(1)} %pad_maximum_fusion), channel_id=1, source_target_pairs={{0,16},{8,72},{16,32},{24,88},{32,48},{40,104},{48,0},{56,120},{64... | collective-permute-start | bytes 4718600 | tf_op jit(solution)/shard_map/ppermute | solution.py:38
  22.9 37.6 %collective-permute-start.12 = (bf16[256,1024]{1,0:T(8,128)(2,1)S(1)}, bf16[256,1024]{1,0:T(8,128)(2,1)S(1)}, u32[]{:S(2)}, u32[]{:S(2)}) collective-permute-start(bf16[256,1024]{1,0:T(8,128)(2,1)S(1)} %convolution_convert_fusion.1), channel_id=1, source_target_pairs={{1,0},{2,1},{3,2},{4,3},{5,4},{6,5},{7,6},{9,8},{10,9},{11,10},{12... | collective-permute-start | bytes 1572872 | tf_op jit(solution)/shard_map/ppermute | solution.py:46
  39.7 15.9 %collective-permute-start.9 = (bf16[512,768]{1,0:T(8,128)(2,1)S(1)}, bf16[512,768]{1,0:T(8,128)(2,1)S(1)}, u32[]{:S(2)}, u32[]{:S(2)}) collective-permute-start(bf16[512,768]{1,0:T(8,128)(2,1)S(1)} %slice.93), channel_id=1, source_target_pairs={{0,48},{8,200},{16,0},{24,216},{32,16},{40,232},{48,32},{56,248},{... | collective-permute-start | bytes 2359304 | tf_op jit(solution)/shard_map/ppermute | solution.py:38
  43.1 12.4 %collective-permute-start.8 = (bf16[512,768]{1,0:T(8,128)(2,1)S(1)}, bf16[512,768]{1,0:T(8,128)(2,1)S(1)}, u32[]{:S(2)}, u32[]{:S(2)}) collective-permute-start(bf16[512,768]{1,0:T(8,128)(2,1)S(1)} %slice.92), channel_id=1, source_target_pairs={{0,16},{8,72},{16,32},{24,88},{32,48},{40,104},{48,0},{56,120},{64... | collective-permute-start | bytes 2359304 | tf_op jit(solution)/shard_map/ppermute | solution.py:38
  44.3 30.8 %collective-permute-start.15 = (bf16[256,2048]{1,0:T(8,128)(2,1)S(1)}, bf16[256,2048]{1,0:T(8,128)(2,1)S(1)}, u32[]{:S(2)}, u32[]{:S(2)}) collective-permute-start(bf16[256,2048]{1,0:T(8,128)(2,1)S(1)} %fusion.4), channel_id=1, source_target_pairs={{1,0},{2,1},{3,2},{4,3},{5,4},{6,5},{7,6},{9,8},{10,9},{11,10},{12... | collective-permute-start | bytes 3145736 | tf_op jit(solution)/shard_map/ppermute | solution.py:46
  45.6 16.6 %collective-permute-start.7 = (bf16[256,1792]{1,0:T(8,128)(2,1)S(1)}, bf16[256,1792]{1,0:T(8,128)(2,1)S(1)}, u32[]{:S(2)}, u32[]{:S(2)}) collective-permute-start(bf16[256,1792]{1,0:T(8,128)(2,1)S(1)} %get-tuple-element.28), channel_id=1, source_target_pairs={{0,48},{8,200},{16,0},{24,216},{32,16},{40,232},{48,32},{56,248},{... | collective-permute-start | bytes 2752520 | tf_op jit(solution)/shard_map/ppermute | solution.py:38
  56.3 8.9 %copy-start.3 = (bf16[1,128,768]{2,1,0:T(8,128)(2,1)S(1)}, bf16[1,128,768]{2,1,0:T(8,128)(2,1)}, u32[]{:S(2)}) copy-start(bf16[1,128,768]{2,1,0:T(8,128)(2,1)} %param.10) | copy-start | bytes 589828
  56.3 8.9 %copy-start.4 = (f32[1,128,192]{1,2,0:T(8,128)S(1)}, f32[1,128,192]{1,2,0:T(8,128)}, u32[]{:S(2)}) copy-start(f32[1,128,192]{1,2,0:T(8,128)} %param.11) | copy-start | bytes 294916
  56.9 8.3 %copy-start.1 = (bf16[1,128,12288]{2,1,0:T(8,128)(2,1)S(1)}, bf16[1,128,12288]{2,1,0:T(8,128)(2,1)}, u32[]{:S(2)}) copy-start(bf16[1,128,12288]{2,1,0:T(8,128)(2,1)} %param.13) | copy-start | bytes 9437188
  57.0 8.2 %collective-permute-start.10 = (f32[128,768]{1,0:T(8,128)S(1)}, f32[128,768]{1,0:T(8,128)S(1)}, u32[]{:S(2)}, u32[]{:S(2)}) collective-permute-start(f32[128,768]{1,0:T(8,128)S(1)} %slice.95), channel_id=1, source_target_pairs={{0,8},{8,0},{1,9},{9,1},{2,10},{10,2},{3,11},{11,3},{4,12},{12,4},... | collective-permute-start | bytes 1179656 | tf_op jit(solution)/shard_map/ppermute | solution.py:42
  60.2 18.4 %collective-permute-start.11 = (bf16[256,1792]{1,0:T(8,128)(2,1)S(1)}, bf16[256,1792]{1,0:T(8,128)(2,1)S(1)}, u32[]{:S(2)}, u32[]{:S(2)}) collective-permute-start(bf16[256,1792]{1,0:T(8,128)(2,1)S(1)} %get-tuple-element.30), channel_id=1, source_target_pairs={{0,16},{8,72},{16,32},{24,88},{32,48},{40,104},{48,0},{56,120},{64... | collective-permute-start | bytes 2752520 | tf_op jit(solution)/shard_map/ppermute | solution.py:38
  60.6 4.7 %copy-start = (bf16[1,128,12288]{2,1,0:T(8,128)(2,1)S(1)}, bf16[1,128,12288]{2,1,0:T(8,128)(2,1)}, u32[]{:S(2)}) copy-start(bf16[1,128,12288]{2,1,0:T(8,128)(2,1)} %param.9) | copy-start | bytes 9437188
  60.6 4.7 %copy-start.5 = (f32[1,192]{1,0:T(1,128)S(1)}, f32[1,192]{1,0:T(1,128)}, u32[]{:S(2)}) copy-start(f32[1,192]{1,0:T(1,128)} %alog_ref.3) | copy-start | bytes 2308
  60.6 1.6 %collective-permute-start.13 = (bf16[128,1024]{1,0:T(8,128)(2,1)S(1)}, bf16[128,1024]{1,0:T(8,128)(2,1)S(1)}, u32[]{:S(2)}, u32[]{:S(2)}) collective-permute-start(bf16[128,1024]{1,0:T(8,128)(2,1)S(1)} %slice.79), channel_id=1, source_target_pairs={{0,8},{8,0},{1,9},{9,1},{2,10},{10,2},{3,11},{11,3},{4,12},{12,4},... | collective-permute-start | bytes 786440 | tf_op jit(solution)/shard_map/ppermute | solution.py:42
  62.2 21.9 %collective-permute-start.14 = (bf16[256,1792]{1,0:T(8,128)(2,1)S(1)}, bf16[256,1792]{1,0:T(8,128)(2,1)S(1)}, u32[]{:S(2)}, u32[]{:S(2)}) collective-permute-start(bf16[256,1792]{1,0:T(8,128)(2,1)S(1)} %get-tuple-element.33), channel_id=1, source_target_pairs={{0,32},{8,136},{16,48},{24,152},{32,0},{40,168},{48,16},{56,184},{... | collective-permute-start | bytes 2752520 | tf_op jit(solution)/shard_map/ppermute | solution.py:38
  75.1 9.7 %collective-permute-start.16 = (bf16[128,2048]{1,0:T(8,128)(2,1)S(1)}, bf16[128,2048]{1,0:T(8,128)(2,1)S(1)}, u32[]{:S(2)}, u32[]{:S(2)}) collective-permute-start(bf16[128,2048]{1,0:T(8,128)(2,1)S(1)} %slice.83), channel_id=1, source_target_pairs={{0,8},{8,0},{1,9},{9,1},{2,10},{10,2},{3,11},{11,3},{4,12},{12,4},... | collective-permute-start | bytes 1572872 | tf_op jit(solution)/shard_map/ppermute | solution.py:42
  77.3 15.7 %collective-permute-start.20 = (bf16[256,1024]{1,0:T(8,128)(2,1)S(1)}, bf16[256,1024]{1,0:T(8,128)(2,1)S(1)}, u32[]{:S(2)}, u32[]{:S(2)}) collective-permute-start(bf16[256,1024]{1,0:T(8,128)(2,1)S(1)} %convolution_convert_fusion), channel_id=1, source_target_pairs={{1,0},{2,1},{3,2},{4,3},{5,4},{6,5},{7,6},{9,8},{10,9},{11,10},{12... | collective-permute-start | bytes 1572872 | tf_op jit(solution)/shard_map/ppermute | solution.py:46
  84.9 12.2 %collective-permute-start.19 = (bf16[256,768]{1,0:T(8,128)(2,1)S(1)}, bf16[256,768]{1,0:T(8,128)(2,1)S(1)}, u32[]{:S(2)}, u32[]{:S(2)}) collective-permute-start(bf16[256,768]{1,0:T(8,128)(2,1)S(1)} %get-tuple-element.44), channel_id=1, source_target_pairs={{0,128},{8,40},{16,144},{24,56},{32,160},{40,8},{48,176},{56,24},{... | collective-permute-start | bytes 1179656 | tf_op jit(solution)/shard_map/ppermute | solution.py:38
  85.1 12.4 %collective-permute-start.18 = (bf16[256,768]{1,0:T(8,128)(2,1)S(1)}, bf16[256,768]{1,0:T(8,128)(2,1)S(1)}, u32[]{:S(2)}, u32[]{:S(2)}) collective-permute-start(bf16[256,768]{1,0:T(8,128)(2,1)S(1)} %get-tuple-element.45), channel_id=1, source_target_pairs={{0,64},{8,24},{16,80},{24,40},{32,96},{40,56},{48,112},{56,8},{64,... | collective-permute-start | bytes 1179656 | tf_op jit(solution)/shard_map/ppermute | solution.py:38
  85.1 12.3 %collective-permute-start.17 = (bf16[256,768]{1,0:T(8,128)(2,1)S(1)}, bf16[256,768]{1,0:T(8,128)(2,1)S(1)}, u32[]{:S(2)}, u32[]{:S(2)}) collective-permute-start(bf16[256,768]{1,0:T(8,128)(2,1)S(1)} %get-tuple-element.46), channel_id=1, source_target_pairs={{0,192},{8,56},{16,208},{24,8},{32,224},{40,24},{48,240},{56,40},{... | collective-permute-start | bytes 1179656 | tf_op jit(solution)/shard_map/ppermute | solution.py:38
  93.0 1.9 %collective-permute-start.21 = (bf16[128,1024]{1,0:T(8,128)(2,1)S(1)}, bf16[128,1024]{1,0:T(8,128)(2,1)S(1)}, u32[]{:S(2)}, u32[]{:S(2)}) collective-permute-start(bf16[128,1024]{1,0:T(8,128)(2,1)S(1)} %slice.97), channel_id=1, source_target_pairs={{0,8},{8,0},{1,9},{9,1},{2,10},{10,2},{3,11},{11,3},{4,12},{12,4},... | collective-permute-start | bytes 786440 | tf_op jit(solution)/shard_map/ppermute | solution.py:42
where the time goes:
time: 100 us; the launch traced here: 98.3 us
  waiting for transfers between devices  32.9 us (33%)
  starting transfers between devices  30.9 us (31%)
  Pallas kernels  22.8 us (23%)
  matrix products  7.12 us (7%)
  local copies, waits for them, and re-layouts  2.3 us (2%)
  other arithmetic  1.34 us (1%)
  between operations  1.01 us (1%)
    ppermute x13, waiting for transfers between devices, ring_shift(): return lax.ppermute(shard, ('x', 'y', 'core'), pairs)  25.5 us
    ppermute x13, starting transfers between devices, ring_shift(): return lax.ppermute(shard, ('x', 'y', 'core'), pairs)  19.9 us
    pallas_call x1, Pallas kernels, scan_grad_b(): pl.pallas_call(grad_b_kernel, grid=(GROUPS,), in_specs=[BY_HEADS, BY_HEAD...  10 us
    pallas_call x1, Pallas kernels, scan_step_grad(): pl.pallas_call(step_grad_kernel, grid=(GROUPS,), in_specs=[BY_HEADS, BY_H...  9.81 us
    ppermute x6, starting transfers between devices, swap_cores(): return lax.ppermute(shard, 'core', [(0, 1), (1, 0)])  7.14 us
    ppermute x3, waiting for transfers between devices, to_previous_section(): lax.ppermute(shard, 'section', [(s, s - 1) for s in range(1, lax.axis_siz...  5.28 us
    ppermute x3, starting transfers between devices, to_previous_section(): lax.ppermute(shard, 'section', [(s, s - 1) for s in range(1, lax.axis_siz...  3.88 us
    dot_general x4, matrix products, outer_dot(): lax.dot_general(a, b, (((0,), (0,)), ((), ())), preferred_element_type=F32)  2.57 us
  transfers between devices with their start and end apart: 22, of which 7 were waited for; matrix products, arithmetic and copies ran while one was open for 8% of the time, Pallas kernels for 23%

commit v1 on v0

--- a/solution.py
+++ b/solution.py
@@ -113,7 +113,7 @@
     return rows, lanes
 
 
-def prepare(step_ref, alog_ref, rate_t, parts, left, right):
+def prepare(step_ref, alog_ref, rate_t, parts, left, right, first=0):
     rows, lanes = iotas()
 
     @pl.when(pl.program_id(0) == 0)
@@ -128,7 +128,7 @@
             right[TOK:, at] = jnp.where(chosen, 1.0, 0.0).astype(BF16)
 
     upper = (rows <= lanes).astype(F32)
-    rates = rate_t[group_rows(), :]
+    rates = rate_t[group_rows(first), :]
     cumul = jnp.dot(
         step_ref[...] * (rates * -LOG2E), upper, precision=HP, preferred_element_type=F32
     )
@@ -168,8 +168,8 @@
             yield h, products[:, k * TOK : (k + 1) * TOK], step_ref[h : h + 1, :]
 
 
-def group_rows():
-    return pl.ds(pl.multiple_of(pl.program_id(0) * PER_GROUP, PER_GROUP), PER_GROUP)
+def group_rows(first):
+    return pl.ds(pl.multiple_of((pl.program_id(0) + first) * PER_GROUP, PER_GROUP), PER_GROUP)
 
 
 def sum_of_heads(x_ref, grad_ref, c_ref, step_ref, left, right, out_ref):
@@ -191,9 +191,9 @@
 
 
 def step_grad_kernel(
-    x_ref, grad_ref, c_ref, b_ref, step_ref, alog_ref, out_ref, rate_t, parts, left, right, direct
+    first, x_ref, grad_ref, c_ref, b_ref, step_ref, alog_ref, out_ref, rate_t, parts, left, right, direct
 ):
-    rates = prepare(step_ref, alog_ref, rate_t, parts, left, right)
+    rates = prepare(step_ref, alog_ref, rate_t, parts, left, right, first)
     rows, lanes = iotas()
     scores = lax.dot_general(
         c_ref[...], b_ref[...], (((1,), (1,)), ((), ())), preferred_element_type=F32
@@ -236,13 +236,18 @@
     )(x, grad, c, steps_t, a_log)
 
 
-def scan_step_grad(x, grad, c, b, steps_t, a_log):
+def scan_step_grad(x, grad, c, b, steps_t, a_log, first, count):
+    by_heads = pl.BlockSpec((TOK, WIDE), lambda g: (0, g + first))
+    by_group = pl.BlockSpec((TOK, STATE), lambda g: (0, g + first))
     return pl.pallas_call(
-        step_grad_kernel,
-        grid=(GROUPS,),
-        in_specs=[BY_HEADS, BY_HEADS, BY_GROUP, BY_GROUP, STEP_ROWS, WHOLE_RATE],
+        functools.partial(step_grad_kernel, first),
+        grid=(count,),
+        in_specs=[
+            by_heads, by_heads, by_group, by_group,
+            pl.BlockSpec((PER_GROUP, TOK), lambda g: (g + first, 0)), WHOLE_RATE,
+        ],
         out_specs=STEP_ROWS,
-        out_shape=jax.ShapeDtypeStruct((HEADS, TOK), F32),
+        out_shape=jax.ShapeDtypeStruct((count * PER_GROUP, TOK), F32),
         scratch_shapes=SCAN_SCRATCH + [pltpu.VMEM((PER_GROUP, TOK), F32)],
         cost_estimate=SMALL_COST,
         compiler_params=pltpu.CompilerParams(vmem_limit_bytes=VMEM_LIMIT),
@@ -276,14 +281,18 @@
     grad_b = scan_grad_b(x, grad, c, steps_t, a_log)
     near = jnp.concatenate([part] + after(near, grad_b))
     far = [ring_shift(near, False, by) for by in (1, -1)]
-    both_b = jnp.concatenate([grad_b, swap_cores(grad_b)])
-
-    def pass_on(rows, *done):
-        both = after(to_previous_section(against_rows(both_b, rows)), *done)
+    other_b = swap_cores(grad_b)
+    both_b = jnp.concatenate([grad_b, other_b])
+
+    def pass_on(rows):
+        return to_previous_section(against_rows(both_b, rows))
+
+    def both_columns(both):
         return both, swap_cores(both[TOK:])
 
-    passed = [pass_on(near, far)]
-    kept, sent = split_columns(after(where, both_b), hidden)
+    near_passed = pass_on(near)
+    kept, sent = split_columns(where, hidden)
+    passed = [both_columns(after(near_passed, far))]
     both_hidden = jnp.concatenate([kept, swap_cores(sent)])
 
     half = block // 2
@@ -295,19 +304,19 @@
     def payload(i):
         return jnp.concatenate([columns(i), both_b], axis=1)
 
-    sends = after([payload(1), payload(2)], far)
+    sends = after([payload(1), payload(2)], far, passed[0][0])
     arrived = [ring_shift(p, False, by) for p, by in zip(sends, (-1, 1))]
-    arrived.append(ring_shift(after(payload(3), last, passed[0], arrived[0]), False, 2))
+    arrived.append(ring_shift(after(payload(3), last, arrived), False, 2))
 
     proj = jnp.zeros((2 * TOK, GROUPS * STATE), F32)
     for i, rows in enumerate((near, *far, last)):
         proj += rows_dot(columns(i), rows)
     proj_b = (proj[:TOK] + swap_cores(proj[TOK:])).astype(BF16)
-    step_grads_t = scan_step_grad(x, grad, c, proj_b, steps_t, a_log)
-
-    arrived = [after(p, step_grads_t) for p in arrived]
-    passed.append(pass_on(jnp.concatenate(far), step_grads_t))
-    passed.append(pass_on(after(last, passed[1][0])))
+    cut = GROUPS // 2
+    early_grads = scan_step_grad(x, grad, c, proj_b, steps_t, a_log, 0, cut)
+    passed.append(both_columns(after(pass_on(jnp.concatenate(far)), early_grads)))
+    last_passed = pass_on(after(last, passed[1][0]))
+    arrived = [after(p, early_grads) for p in arrived]
     sums = outer_dot(columns(0), both_b)
     for p in arrived:
         sums += outer_dot(p[:, :block], p[:, block:])
@@ -315,10 +324,15 @@
     shifts = ((1, -1), (2, 1), (3, 2))
     others = [ring_shift(parts[i * SHARD : (i + 1) * SHARD], True, by) for i, by in shifts]
 
+    late_b = after(proj_b, parts)
+    late_grads = scan_step_grad(x, grad, c, late_b, steps_t, a_log, cut, GROUPS - cut)
+    step_grads_t = jnp.concatenate([early_grads, late_grads])
+    passed.append(both_columns(after(last_passed, late_grads)))
+
     orders = (tuple(range(RING)), tuple(range(RING, 3 * RING)), tuple(range(3 * RING, 4 * RING)))
     joined = join_columns(where, passed[0] + passed[1] + passed[2], orders, hidden.shape[1])
     weight_grads = sums[:SHARD]
-    for other in after(others, joined):
+    for other in after(others, joined, step_grads_t):
         weight_grads += other.astype(F32)
     return weight_grads.astype(BF16)[None], joined[None], step_grads_t.T[None]
 

time: 100 us -> 97.9 us (0.979); the launches traced: 98.3 us -> 97.7 us
  waiting for transfers between devices: 32.9 us -> 29 us
  starting transfers between devices: 30.9 us -> 33.8 us
    ppermute x3, waiting for transfers between devices: 5.28 us -> 0.21 us  [to_previous_section(): lax.ppermute(shard, 'section', [(s, s - 1) for s in range(1, lax.axis_siz...]
    ppermute x6, starting transfers between devices: 7.14 us -> 11.6 us  [swap_cores(): return lax.ppermute(shard, 'core', [(0, 1), (1, 0)])]
    ppermute x13, waiting for transfers between devices: 25.5 us -> 28.3 us  [ring_shift(): return lax.ppermute(shard, ('x', 'y', 'core'), pairs)]
    ppermute x6, waiting for transfers between devices: 2.07 us -> 0.53 us  [swap_cores(): return lax.ppermute(shard, 'core', [(0, 1), (1, 0)])]
    ppermute x13, starting transfers between devices: 19.9 us -> 18.4 us  [ring_shift(): return lax.ppermute(shard, ('x', 'y', 'core'), pairs)]
    pallas_call x1 -> x2, Pallas kernels: 9.81 us -> 9.4 us  [scan_step_grad(): pl.pallas_call(functools.partial(step_grad_kernel, first), grid=(count,),...]
  transfers between devices with their start and end apart: 22 -> 22, of which waited for: 7 -> 8; matrix products, arithmetic and copies ran while one was open for 8% -> 9% of each run, Pallas kernels for 23% -> 23%
where the time goes in v1:
time: 97.9 us; the launch traced here: 97.7 us
  starting transfers between devices  33.8 us (35%)
  waiting for transfers between devices  29 us (30%)
  Pallas kernels  22.4 us (23%)
  matrix products  7.16 us (7%)
  local copies, waits for them, and re-layouts  2.3 us (2%)
  other arithmetic  2 us (2%)
  between operations  1.02 us (1%)
    ppermute x13, waiting for transfers between devices, ring_shift(): return lax.ppermute(shard, ('x', 'y', 'core'), pairs)  28.3 us
    ppermute x13, starting transfers between devices, ring_shift(): return lax.ppermute(shard, ('x', 'y', 'core'), pairs)  18.4 us
    ppermute x6, starting transfers between devices, swap_cores(): return lax.ppermute(shard, 'core', [(0, 1), (1, 0)])  11.6 us
    pallas_call x1, Pallas kernels, scan_grad_b(): pl.pallas_call(grad_b_kernel, grid=(GROUPS,), in_specs=[BY_HEADS, BY_HEAD...  10 us
    pallas_call x2, Pallas kernels, scan_step_grad(): pl.pallas_call(functools.partial(step_grad_kernel, first), grid=(count,),...  9.4 us
    ppermute x3, starting transfers between devices, to_previous_section(): lax.ppermute(shard, 'section', [(s, s - 1) for s in range(1, lax.axis_siz...  3.88 us
    dot_general x4, matrix products, outer_dot(): lax.dot_general(a, b, (((0,), (0,)), ((), ())), preferred_element_type=F32)  2.57 us
    dot_general x4, matrix products, rows_dot(): return jnp.dot(a, b, preferred_element_type=F32)  2.36 us
  transfers between devices with their start and end apart: 22, of which 8 were waited for; matrix products, arithmetic and copies ran while one was open for 9% of the time, Pallas kernels for 23%

profile of v1, /device:TPU:1, one launch (start us, length us, event | category | flops | bytes accessed | tf_op | source)
XLA Modules:
  0.0 97.7 jit_solution(6682037736582601759)
XLA Ops:
  0.6 3.8 %collective-permute-start.4 = (bf16[256,768]{1,0:T(8,128)(2,1)}, bf16[256,768]{1,0:T(8,128)(2,1)S(1)}, u32[]{:S(2)}, u32[]{:S(2)}) collective-permute-start(bf16[256,768]{1,0:T(8,128)(2,1)} %bitcast.38), channel_id=1, source_target_pairs={{0,128},{8,40},{16,144},{24,56},{32,160},{40,8},{48,176},{56,24},{... | collective-permute-start | bytes 1179656 | tf_op jit(solution)/shard_map/ppermute | solution.py:38
  4.5 0.8 collective-permute-start.3
  5.2 0.7 collective-permute-start.2
  6.0 1.6 %copy-done.2 = bf16[1,128,8192]{2,1,0:T(8,128)(2,1)S(1)} copy-done((bf16[1,128,8192]{2,1,0:T(8,128)(2,1)S(1)}, bf16[1,128,8192]{2,1,0:T(8,128)(2,1)}, u32[]{:S(2)}) %copy-start.2) | copy-done | bytes 2097176
  7.6 0.8 split_columns.1
  8.4 1.4 %collective-permute-start = (bf16[128,4096]{1,0:T(8,128)(2,1)S(1)}, bf16[128,4096]{1,0:T(8,128)(2,1)S(1)}, u32[]{:S(2)}, u32[]{:S(2)}) collective-permute-start(bf16[128,4096]{1,0:T(8,128)(2,1)S(1)} %get-tuple-element.24), channel_id=1, source_target_pairs={{0,8},{8,0},{1,9},{9,1},{2,10},{10,2},{3,11},{11,3},{4,12},{12,4},... | collective-permute-start | bytes 3145736 | tf_op jit(solution)/shard_map/ppermute | solution.py:42
  9.9 10.0 %scan_grad_b.1 = bf16[128,768]{1,0:T(8,128)(2,1)} custom-call(bf16[128,12288]{1,0:T(8,128)(2,1)} %bitcast.24, bf16[128,12288]{1,0:T(8,128)(2,1)} %bitcast.27, bf16[128,768]{1,0:T(8,128)(2,1)} %bitcast.31, f32[192,128]{1,0:T(8,128)} %bitcast.34, f32[1,192]{1,0:T(1,128)} %alog_ref.5), custom_call_target="tpu_custom_call" | custom-call | bytes 1024 | tf_op jit(solution)/shard_map/scan_grad_b/pallas_call | solution.py:226
  20.0 2.1 %collective-permute-start.6 = (bf16[1024,768]{1,0:T(8,128)(2,1)S(1)}, bf16[1024,768]{1,0:T(8,128)(2,1)S(1)}, u32[]{:S(2)}, u32[]{:S(2)}) collective-permute-start(bf16[1024,768]{1,0:T(8,128)(2,1)S(1)} %pad_maximum_fusion), channel_id=1, source_target_pairs={{0,48},{8,200},{16,0},{24,216},{32,16},{40,232},{48,32},{56,248},{... | collective-permute-start | bytes 4718600 | tf_op jit(solution)/shard_map/ppermute | solution.py:38
  22.9 1.3 %collective-permute-start.7 = (bf16[256,1024]{1,0:T(8,128)(2,1)S(1)}, bf16[256,1024]{1,0:T(8,128)(2,1)S(1)}, u32[]{:S(2)}, u32[]{:S(2)}) collective-permute-start(bf16[256,1024]{1,0:T(8,128)(2,1)S(1)} %convolution_convert_fusion.1), channel_id=1, source_target_pairs={{1,0},{2,1},{3,2},{4,3},{5,4},{6,5},{7,6},{9,8},{10,9},{11,10},{12... | collective-permute-start | bytes 1572872 | tf_op jit(solution)/shard_map/ppermute | solution.py:46
  24.6 15.0 %collective-permute-done.6 = bf16[1024,768]{1,0:T(8,128)(2,1)S(1)} collective-permute-done((bf16[1024,768]{1,0:T(8,128)(2,1)S(1)}, bf16[1024,768]{1,0:T(8,128)(2,1)S(1)}, u32[]{:S(2)}, u32[]{:S(2)}) %collective-permute-start.6) | collective-permute-done | bytes 1572896 | tf_op jit(solution)/shard_map/ppermute | solution.py:38
  39.7 3.4 %collective-permute-start.10 = (bf16[512,768]{1,0:T(8,128)(2,1)S(1)}, bf16[512,768]{1,0:T(8,128)(2,1)S(1)}, u32[]{:S(2)}, u32[]{:S(2)}) collective-permute-start(bf16[512,768]{1,0:T(8,128)(2,1)S(1)} %slice.93), channel_id=1, source_target_pairs={{0,48},{8,200},{16,0},{24,216},{32,16},{40,232},{48,32},{56,248},{... | collective-permute-start | bytes 2359304 | tf_op jit(solution)/shard_map/ppermute | solution.py:38
  43.2 1.0 %fusion.4 = bf16[256,2048]{1,0:T(8,128)(2,1)S(1)} fusion(bf16[1024,768]{1,0:T(8,128)(2,1)S(1)} %collective-permute-done.6, bf16[1024,768]{1,0:T(8,128)(2,1)S(1)} %collective-permute-done.5, bf16[128,768]{1,0:T(8,128)(2,1)S(1)} %collective-permute-done.1, bf16[128,768]{1,0:T(8,128)(2,1)S(1)} %copy-done.6), kind=kOutput, calls=%fused_computation.5 | convolution fusion | flops 812908544 | bytes 4587520 | tf_op jit(solution)/shard_map/dot_general | solution.py:267
  44.3 1.3 %collective-permute-start.15 = (bf16[256,2048]{1,0:T(8,128)(2,1)S(1)}, bf16[256,2048]{1,0:T(8,128)(2,1)S(1)}, u32[]{:S(2)}, u32[]{:S(2)}) collective-permute-start(bf16[256,2048]{1,0:T(8,128)(2,1)S(1)} %fusion.4), channel_id=1, source_target_pairs={{1,0},{2,1},{3,2},{4,3},{5,4},{6,5},{7,6},{9,8},{10,9},{11,10},{12... | collective-permute-start | bytes 3145736 | tf_op jit(solution)/shard_map/ppermute | solution.py:46
  45.6 2.7 %collective-permute-start.8 = (bf16[256,1792]{1,0:T(8,128)(2,1)S(1)}, bf16[256,1792]{1,0:T(8,128)(2,1)S(1)}, u32[]{:S(2)}, u32[]{:S(2)}) collective-permute-start(bf16[256,1792]{1,0:T(8,128)(2,1)S(1)} %get-tuple-element.29), channel_id=1, source_target_pairs={{0,48},{8,200},{16,0},{24,216},{32,16},{40,232},{48,32},{56,248},{... | collective-permute-start | bytes 2752520 | tf_op jit(solution)/shard_map/ppermute | solution.py:38
  49.5 6.1 %collective-permute-done.9 = bf16[512,768]{1,0:T(8,128)(2,1)S(1)} collective-permute-done((bf16[512,768]{1,0:T(8,128)(2,1)S(1)}, bf16[512,768]{1,0:T(8,128)(2,1)S(1)}, u32[]{:S(2)}, u32[]{:S(2)}) %collective-permute-start.9) | collective-permute-done | bytes 786464 | tf_op jit(solution)/shard_map/ppermute | solution.py:38
  56.3 0.6 fusion.8
  57.0 3.2 %collective-permute-start.11 = (f32[128,768]{1,0:T(8,128)S(1)}, f32[128,768]{1,0:T(8,128)S(1)}, u32[]{:S(2)}, u32[]{:S(2)}) collective-permute-start(f32[128,768]{1,0:T(8,128)S(1)} %slice.95), channel_id=1, source_target_pairs={{0,8},{8,0},{1,9},{9,1},{2,10},{10,2},{3,11},{11,3},{4,12},{12,4},... | collective-permute-start | bytes 1179656 | tf_op jit(solution)/shard_map/ppermute | solution.py:42
  61.0 0.8 collective-permute-done.8
  61.9 3.5 %collective-permute-done.12 = bf16[256,1792]{1,0:T(8,128)(2,1)S(1)} collective-permute-done((bf16[256,1792]{1,0:T(8,128)(2,1)S(1)}, bf16[256,1792]{1,0:T(8,128)(2,1)S(1)}, u32[]{:S(2)}, u32[]{:S(2)}) %collective-permute-start.12) | collective-permute-done | bytes 917536 | tf_op jit(solution)/shard_map/ppermute | solution.py:38
  65.5 4.7 %scan_step_grad.2 = f32[96,128]{1,0:T(8,128)S(1)} custom-call(bf16[128,12288]{1,0:T(8,128)(2,1)S(1)} %bitcast.25, bf16[128,12288]{1,0:T(8,128)(2,1)S(1)} %bitcast.28, bf16[128,768]{1,0:T(8,128)(2,1)S(1)} %bitcast.32, bf16[128,768]{1,0:T(8,128)(2,1)S(1)} %fusion.21.b_ref, f32[192,128]{1,0:T(8,128)S(1)} %bitcast.35, f32[1,192]{1,0:T(1,128)S(1)} %copy-done.5), custom_call_target="tpu_custom_call" | custom-call | bytes 1024 | tf_op jit(solution)/shard_map/scan_step_grad/pallas_call | solution.py:242
  70.3 3.2 %collective-permute-start.16 = (bf16[128,2048]{1,0:T(8,128)(2,1)S(1)}, bf16[128,2048]{1,0:T(8,128)(2,1)S(1)}, u32[]{:S(2)}, u32[]{:S(2)}) collective-permute-start(bf16[128,2048]{1,0:T(8,128)(2,1)S(1)} %slice.83), channel_id=1, source_target_pairs={{0,8},{8,0},{1,9},{9,1},{2,10},{10,2},{3,11},{11,3},{4,12},{12,4},... | collective-permute-start | bytes 1572872 | tf_op jit(solution)/shard_map/ppermute | solution.py:42
  74.2 1.3 %collective-permute-start.20 = (bf16[256,1024]{1,0:T(8,128)(2,1)S(1)}, bf16[256,1024]{1,0:T(8,128)(2,1)S(1)}, u32[]{:S(2)}, u32[]{:S(2)}) collective-permute-start(bf16[256,1024]{1,0:T(8,128)(2,1)S(1)} %convolution_convert_fusion), channel_id=1, source_target_pairs={{1,0},{2,1},{3,2},{4,3},{5,4},{6,5},{7,6},{9,8},{10,9},{11,10},{12... | collective-permute-start | bytes 1572872 | tf_op jit(solution)/shard_map/ppermute | solution.py:46
  76.7 2.7 %collective-permute-done.13 = bf16[256,1792]{1,0:T(8,128)(2,1)S(1)} collective-permute-done((bf16[256,1792]{1,0:T(8,128)(2,1)S(1)}, bf16[256,1792]{1,0:T(8,128)(2,1)S(1)}, u32[]{:S(2)}, u32[]{:S(2)}) %collective-permute-start.13) | collective-permute-done | bytes 917536 | tf_op jit(solution)/shard_map/ppermute | solution.py:38
  79.4 0.7 fusion.35
  80.3 2.1 %collective-permute-start.19 = (bf16[256,768]{1,0:T(8,128)(2,1)S(1)}, bf16[256,768]{1,0:T(8,128)(2,1)S(1)}, u32[]{:S(2)}, u32[]{:S(2)}) collective-permute-start(bf16[256,768]{1,0:T(8,128)(2,1)S(1)} %get-tuple-element.46), channel_id=1, source_target_pairs={{0,128},{8,40},{16,144},{24,56},{32,160},{40,8},{48,176},{56,24},{... | collective-permute-start | bytes 1179656 | tf_op jit(solution)/shard_map/ppermute | solution.py:38
  82.4 1.0 %collective-permute-start.18 = (bf16[256,768]{1,0:T(8,128)(2,1)S(1)}, bf16[256,768]{1,0:T(8,128)(2,1)S(1)}, u32[]{:S(2)}, u32[]{:S(2)}) collective-permute-start(bf16[256,768]{1,0:T(8,128)(2,1)S(1)} %get-tuple-element.47), channel_id=1, source_target_pairs={{0,64},{8,24},{16,80},{24,40},{32,96},{40,56},{48,112},{56,8},{64,... | collective-permute-start | bytes 1179656 | tf_op jit(solution)/shard_map/ppermute | solution.py:38
  83.4 1.7 %collective-permute-start.17 = (bf16[256,768]{1,0:T(8,128)(2,1)S(1)}, bf16[256,768]{1,0:T(8,128)(2,1)S(1)}, u32[]{:S(2)}, u32[]{:S(2)}) collective-permute-start(bf16[256,768]{1,0:T(8,128)(2,1)S(1)} %get-tuple-element.48), channel_id=1, source_target_pairs={{0,192},{8,56},{16,208},{24,8},{32,224},{40,24},{48,240},{56,40},{... | collective-permute-start | bytes 1179656 | tf_op jit(solution)/shard_map/ppermute | solution.py:38
  85.0 4.7 %scan_step_grad.3 = f32[96,128]{1,0:T(8,128)S(1)} custom-call(bf16[128,12288]{1,0:T(8,128)(2,1)S(1)} %bitcast.26, bf16[128,12288]{1,0:T(8,128)(2,1)S(1)} %bitcast.29, bf16[128,768]{1,0:T(8,128)(2,1)S(1)} %bitcast.33, bf16[128,768]{1,0:T(8,128)(2,1)S(1)} %fusion.21.b_ref, f32[192,128]{1,0:T(8,128)S(1)} %bitcast.36, f32[1,192]{1,0:T(1,128)S(1)} %copy-done.5), custom_call_target="tpu_custom_call" | custom-call | bytes 1024 | tf_op jit(solution)/shard_map/scan_step_grad/pallas_call | solution.py:242
  89.9 3.5 %collective-permute-start.21 = (bf16[128,1024]{1,0:T(8,128)(2,1)S(1)}, bf16[128,1024]{1,0:T(8,128)(2,1)S(1)}, u32[]{:S(2)}, u32[]{:S(2)}) collective-permute-start(bf16[128,1024]{1,0:T(8,128)(2,1)S(1)} %slice.87), channel_id=1, source_target_pairs={{0,8},{8,0},{1,9},{9,1},{2,10},{10,2},{3,11},{11,3},{4,12},{12,4},... | collective-permute-start | bytes 786440 | tf_op jit(solution)/shard_map/ppermute | solution.py:42
  93.4 0.6 fusion.26
  94.6 2.1 %join_columns.1 = bf16[128,8192]{1,0:T(8,128)(2,1)} custom-call(s32[3]{0:T(128)S(1)} %pad_add_fusion.where_ref, bf16[256,1024]{1,0:T(8,128)(2,1)S(1)} %collective-permute-done.7.refs_0_, bf16[128,1024]{1,0:T(8,128)(2,1)S(1)} %collective-permute-done.14.refs_1_, bf16[256,2048]{1,0:T(8,128)(2,1)S(1)} %collective-permute-done.15.refs_2_, ...), custom_call_target="tpu_custom_call" | custom-call | bytes 1024 | tf_op jit(solution)/shard_map/join_columns/pallas_call | solution.py:98
  96.7 0.9 fusion.20
  (62 shorter events, 6.9 us)
Async XLA Ops:
  0.6 19.3 %collective-permute-start.4 = (bf16[256,768]{1,0:T(8,128)(2,1)}, bf16[256,768]{1,0:T(8,128)(2,1)S(1)}, u32[]{:S(2)}, u32[]{:S(2)}) collective-permute-start(bf16[256,768]{1,0:T(8,128)(2,1)} %bitcast.38), channel_id=1, source_target_pairs={{0,128},{8,40},{16,144},{24,56},{32,160},{40,8},{48,176},{56,24},{... | collective-permute-start | bytes 1179656 | tf_op jit(solution)/shard_map/ppermute | solution.py:38
  4.5 15.5 %collective-permute-start.3 = (bf16[256,768]{1,0:T(8,128)(2,1)}, bf16[256,768]{1,0:T(8,128)(2,1)S(1)}, u32[]{:S(2)}, u32[]{:S(2)}) collective-permute-start(bf16[256,768]{1,0:T(8,128)(2,1)} %bitcast.39), channel_id=1, source_target_pairs={{0,192},{8,56},{16,208},{24,8},{32,224},{40,24},{48,240},{56,40},{... | collective-permute-start | bytes 1179656 | tf_op jit(solution)/shard_map/ppermute | solution.py:38
  5.2 14.7 %collective-permute-start.2 = (bf16[256,768]{1,0:T(8,128)(2,1)}, bf16[256,768]{1,0:T(8,128)(2,1)S(1)}, u32[]{:S(2)}, u32[]{:S(2)}) collective-permute-start(bf16[256,768]{1,0:T(8,128)(2,1)} %bitcast.40), channel_id=1, source_target_pairs={{0,64},{8,24},{16,80},{24,40},{32,96},{40,56},{48,112},{56,8},{64,... | collective-permute-start | bytes 1179656 | tf_op jit(solution)/shard_map/ppermute | solution.py:38
  6.0 1.6 %copy-start.2 = (bf16[1,128,8192]{2,1,0:T(8,128)(2,1)S(1)}, bf16[1,128,8192]{2,1,0:T(8,128)(2,1)}, u32[]{:S(2)}) copy-start(bf16[1,128,8192]{2,1,0:T(8,128)(2,1)} %param.7) | copy-start | bytes 6291460
  8.4 15.8 %collective-permute-start = (bf16[128,4096]{1,0:T(8,128)(2,1)S(1)}, bf16[128,4096]{1,0:T(8,128)(2,1)S(1)}, u32[]{:S(2)}, u32[]{:S(2)}) collective-permute-start(bf16[128,4096]{1,0:T(8,128)(2,1)S(1)} %get-tuple-element.24), channel_id=1, source_target_pairs={{0,8},{8,0},{1,9},{9,1},{2,10},{10,2},{3,11},{11,3},{4,12},{12,4},... | collective-permute-start | bytes 3145736 | tf_op jit(solution)/shard_map/ppermute | solution.py:42
  9.9 10.1 %copy-start.7 = (bf16[1,256,768]{2,1,0:T(8,128)(2,1)S(1)}, bf16[1,256,768]{2,1,0:T(8,128)(2,1)}, u32[]{:S(2)}) copy-start(bf16[1,256,768]{2,1,0:T(8,128)(2,1)} %param.8) | copy-start | bytes 1179652
  19.9 2.4 %copy-start.6 = (bf16[128,768]{1,0:T(8,128)(2,1)S(1)}, bf16[128,768]{1,0:T(8,128)(2,1)}, u32[]{:S(2)}) copy-start(bf16[128,768]{1,0:T(8,128)(2,1)} %scan_grad_b.1) | copy-start | bytes 589828
  19.9 2.4 %collective-permute-start.1 = (bf16[128,768]{1,0:T(8,128)(2,1)}, bf16[128,768]{1,0:T(8,128)(2,1)S(1)}, u32[]{:S(2)}, u32[]{:S(2)}) collective-permute-start(bf16[128,768]{1,0:T(8,128)(2,1)} %scan_grad_b.1), channel_id=1, source_target_pairs={{0,8},{8,0},{1,9},{9,1},{2,10},{10,2},{3,11},{11,3},{4,12},{12,4},... | collective-permute-start | bytes 589832 | tf_op jit(solution)/shard_map/ppermute | solution.py:42
  20.0 19.6 %collective-permute-start.6 = (bf16[1024,768]{1,0:T(8,128)(2,1)S(1)}, bf16[1024,768]{1,0:T(8,128)(2,1)S(1)}, u32[]{:S(2)}, u32[]{:S(2)}) collective-permute-start(bf16[1024,768]{1,0:T(8,128)(2,1)S(1)} %pad_maximum_fusion), channel_id=1, source_target_pairs={{0,48},{8,200},{16,0},{24,216},{32,16},{40,232},{48,32},{56,248},{... | collective-permute-start | bytes 4718600 | tf_op jit(solution)/shard_map/ppermute | solution.py:38
  22.2 20.9 %collective-permute-start.5 = (bf16[1024,768]{1,0:T(8,128)(2,1)S(1)}, bf16[1024,768]{1,0:T(8,128)(2,1)S(1)}, u32[]{:S(2)}, u32[]{:S(2)}) collective-permute-start(bf16[1024,768]{1,0:T(8,128)(2,1)S(1)} %pad_maximum_fusion), channel_id=1, source_target_pairs={{0,16},{8,72},{16,32},{24,88},{32,48},{40,104},{48,0},{56,120},{64... | collective-permute-start | bytes 4718600 | tf_op jit(solution)/shard_map/ppermute | solution.py:38
  22.9 21.4 %collective-permute-start.7 = (bf16[256,1024]{1,0:T(8,128)(2,1)S(1)}, bf16[256,1024]{1,0:T(8,128)(2,1)S(1)}, u32[]{:S(2)}, u32[]{:S(2)}) collective-permute-start(bf16[256,1024]{1,0:T(8,128)(2,1)S(1)} %convolution_convert_fusion.1), channel_id=1, source_target_pairs={{1,0},{2,1},{3,2},{4,3},{5,4},{6,5},{7,6},{9,8},{10,9},{11,10},{12... | collective-permute-start | bytes 1572872 | tf_op jit(solution)/shard_map/ppermute | solution.py:46
  39.7 15.9 %collective-permute-start.10 = (bf16[512,768]{1,0:T(8,128)(2,1)S(1)}, bf16[512,768]{1,0:T(8,128)(2,1)S(1)}, u32[]{:S(2)}, u32[]{:S(2)}) collective-permute-start(bf16[512,768]{1,0:T(8,128)(2,1)S(1)} %slice.93), channel_id=1, source_target_pairs={{0,48},{8,200},{16,0},{24,216},{32,16},{40,232},{48,32},{56,248},{... | collective-permute-start | bytes 2359304 | tf_op jit(solution)/shard_map/ppermute | solution.py:38
  43.1 12.4 %collective-permute-start.9 = (bf16[512,768]{1,0:T(8,128)(2,1)S(1)}, bf16[512,768]{1,0:T(8,128)(2,1)S(1)}, u32[]{:S(2)}, u32[]{:S(2)}) collective-permute-start(bf16[512,768]{1,0:T(8,128)(2,1)S(1)} %slice.92), channel_id=1, source_target_pairs={{0,16},{8,72},{16,32},{24,88},{32,48},{40,104},{48,0},{56,120},{64... | collective-permute-start | bytes 2359304 | tf_op jit(solution)/shard_map/ppermute | solution.py:38
  44.3 26.0 %collective-permute-start.15 = (bf16[256,2048]{1,0:T(8,128)(2,1)S(1)}, bf16[256,2048]{1,0:T(8,128)(2,1)S(1)}, u32[]{:S(2)}, u32[]{:S(2)}) collective-permute-start(bf16[256,2048]{1,0:T(8,128)(2,1)S(1)} %fusion.4), channel_id=1, source_target_pairs={{1,0},{2,1},{3,2},{4,3},{5,4},{6,5},{7,6},{9,8},{10,9},{11,10},{12... | collective-permute-start | bytes 3145736 | tf_op jit(solution)/shard_map/ppermute | solution.py:46
  45.6 16.3 %collective-permute-start.8 = (bf16[256,1792]{1,0:T(8,128)(2,1)S(1)}, bf16[256,1792]{1,0:T(8,128)(2,1)S(1)}, u32[]{:S(2)}, u32[]{:S(2)}) collective-permute-start(bf16[256,1792]{1,0:T(8,128)(2,1)S(1)} %get-tuple-element.29), channel_id=1, source_target_pairs={{0,48},{8,200},{16,0},{24,216},{32,16},{40,232},{48,32},{56,248},{... | collective-permute-start | bytes 2752520 | tf_op jit(solution)/shard_map/ppermute | solution.py:38
  48.3 17.1 %collective-permute-start.12 = (bf16[256,1792]{1,0:T(8,128)(2,1)S(1)}, bf16[256,1792]{1,0:T(8,128)(2,1)S(1)}, u32[]{:S(2)}, u32[]{:S(2)}) collective-permute-start(bf16[256,1792]{1,0:T(8,128)(2,1)S(1)} %get-tuple-element.31), channel_id=1, source_target_pairs={{0,16},{8,72},{16,32},{24,88},{32,48},{40,104},{48,0},{56,120},{64... | collective-permute-start | bytes 2752520 | tf_op jit(solution)/shard_map/ppermute | solution.py:38
  56.3 9.2 %copy-start.3 = (bf16[1,128,768]{2,1,0:T(8,128)(2,1)S(1)}, bf16[1,128,768]{2,1,0:T(8,128)(2,1)}, u32[]{:S(2)}) copy-start(bf16[1,128,768]{2,1,0:T(8,128)(2,1)} %param.10) | copy-start | bytes 589828
  56.3 9.2 %copy-start.4 = (f32[1,128,192]{1,2,0:T(8,128)S(1)}, f32[1,128,192]{1,2,0:T(8,128)}, u32[]{:S(2)}) copy-start(f32[1,128,192]{1,2,0:T(8,128)} %param.11) | copy-start | bytes 294916
  57.0 8.5 %copy-start.1 = (bf16[1,128,12288]{2,1,0:T(8,128)(2,1)S(1)}, bf16[1,128,12288]{2,1,0:T(8,128)(2,1)}, u32[]{:S(2)}) copy-start(bf16[1,128,12288]{2,1,0:T(8,128)(2,1)} %param.13) | copy-start | bytes 9437188
  57.0 8.5 %copy-start = (bf16[1,128,12288]{2,1,0:T(8,128)(2,1)S(1)}, bf16[1,128,12288]{2,1,0:T(8,128)(2,1)}, u32[]{:S(2)}) copy-start(bf16[1,128,12288]{2,1,0:T(8,128)(2,1)} %param.9) | copy-start | bytes 9437188
  57.0 8.5 %copy-start.5 = (f32[1,192]{1,0:T(1,128)S(1)}, f32[1,192]{1,0:T(1,128)}, u32[]{:S(2)}) copy-start(f32[1,192]{1,0:T(1,128)} %alog_ref.5) | copy-start | bytes 2308
  57.0 8.4 %collective-permute-start.11 = (f32[128,768]{1,0:T(8,128)S(1)}, f32[128,768]{1,0:T(8,128)S(1)}, u32[]{:S(2)}, u32[]{:S(2)}) collective-permute-start(f32[128,768]{1,0:T(8,128)S(1)} %slice.95), channel_id=1, source_target_pairs={{0,8},{8,0},{1,9},{9,1},{2,10},{10,2},{3,11},{11,3},{4,12},{12,4},... | collective-permute-start | bytes 1179656 | tf_op jit(solution)/shard_map/ppermute | solution.py:42
  60.9 19.2 %collective-permute-start.14 = (bf16[128,1024]{1,0:T(8,128)(2,1)S(1)}, bf16[128,1024]{1,0:T(8,128)(2,1)S(1)}, u32[]{:S(2)}, u32[]{:S(2)}) collective-permute-start(bf16[128,1024]{1,0:T(8,128)(2,1)S(1)} %slice.82), channel_id=1, source_target_pairs={{0,8},{8,0},{1,9},{9,1},{2,10},{10,2},{3,11},{11,3},{4,12},{12,4},... | collective-permute-start | bytes 786440 | tf_op jit(solution)/shard_map/ppermute | solution.py:42
  65.4 14.0 %collective-permute-start.13 = (bf16[256,1792]{1,0:T(8,128)(2,1)S(1)}, bf16[256,1792]{1,0:T(8,128)(2,1)S(1)}, u32[]{:S(2)}, u32[]{:S(2)}) collective-permute-start(bf16[256,1792]{1,0:T(8,128)(2,1)S(1)} %get-tuple-element.33), channel_id=1, source_target_pairs={{0,32},{8,136},{16,48},{24,152},{32,0},{40,168},{48,16},{56,184},{... | collective-permute-start | bytes 2752520 | tf_op jit(solution)/shard_map/ppermute | solution.py:38
  70.3 9.9 %collective-permute-start.16 = (bf16[128,2048]{1,0:T(8,128)(2,1)S(1)}, bf16[128,2048]{1,0:T(8,128)(2,1)S(1)}, u32[]{:S(2)}, u32[]{:S(2)}) collective-permute-start(bf16[128,2048]{1,0:T(8,128)(2,1)S(1)} %slice.83), channel_id=1, source_target_pairs={{0,8},{8,0},{1,9},{9,1},{2,10},{10,2},{3,11},{11,3},{4,12},{12,4},... | collective-permute-start | bytes 1572872 | tf_op jit(solution)/shard_map/ppermute | solution.py:42
  74.2 15.7 %collective-permute-start.20 = (bf16[256,1024]{1,0:T(8,128)(2,1)S(1)}, bf16[256,1024]{1,0:T(8,128)(2,1)S(1)}, u32[]{:S(2)}, u32[]{:S(2)}) collective-permute-start(bf16[256,1024]{1,0:T(8,128)(2,1)S(1)} %convolution_convert_fusion), channel_id=1, source_target_pairs={{1,0},{2,1},{3,2},{4,3},{5,4},{6,5},{7,6},{9,8},{10,9},{11,10},{12... | collective-permute-start | bytes 1572872 | tf_op jit(solution)/shard_map/ppermute | solution.py:46
  80.3 16.4 %collective-permute-start.19 = (bf16[256,768]{1,0:T(8,128)(2,1)S(1)}, bf16[256,768]{1,0:T(8,128)(2,1)S(1)}, u32[]{:S(2)}, u32[]{:S(2)}) collective-permute-start(bf16[256,768]{1,0:T(8,128)(2,1)S(1)} %get-tuple-element.46), channel_id=1, source_target_pairs={{0,128},{8,40},{16,144},{24,56},{32,160},{40,8},{48,176},{56,24},{... | collective-permute-start | bytes 1179656 | tf_op jit(solution)/shard_map/ppermute | solution.py:38
  82.4 14.3 %collective-permute-start.18 = (bf16[256,768]{1,0:T(8,128)(2,1)S(1)}, bf16[256,768]{1,0:T(8,128)(2,1)S(1)}, u32[]{:S(2)}, u32[]{:S(2)}) collective-permute-start(bf16[256,768]{1,0:T(8,128)(2,1)S(1)} %get-tuple-element.47), channel_id=1, source_target_pairs={{0,64},{8,24},{16,80},{24,40},{32,96},{40,56},{48,112},{56,8},{64,... | collective-permute-start | bytes 1179656 | tf_op jit(solution)/shard_map/ppermute | solution.py:38
  83.4 13.3 %collective-permute-start.17 = (bf16[256,768]{1,0:T(8,128)(2,1)S(1)}, bf16[256,768]{1,0:T(8,128)(2,1)S(1)}, u32[]{:S(2)}, u32[]{:S(2)}) collective-permute-start(bf16[256,768]{1,0:T(8,128)(2,1)S(1)} %get-tuple-element.48), channel_id=1, source_target_pairs={{0,192},{8,56},{16,208},{24,8},{32,224},{40,24},{48,240},{56,40},{... | collective-permute-start | bytes 1179656 | tf_op jit(solution)/shard_map/ppermute | solution.py:38
  89.9 4.7 %collective-permute-start.21 = (bf16[128,1024]{1,0:T(8,128)(2,1)S(1)}, bf16[128,1024]{1,0:T(8,128)(2,1)S(1)}, u32[]{:S(2)}, u32[]{:S(2)}) collective-permute-start(bf16[128,1024]{1,0:T(8,128)(2,1)S(1)} %slice.87), channel_id=1, source_target_pairs={{0,8},{8,0},{1,9},{9,1},{2,10},{10,2},{3,11},{11,3},{4,12},{12,4},... | collective-permute-start | bytes 786440 | tf_op jit(solution)/shard_map/ppermute | solution.py:42

commit v2 on v1

--- a/solution.py
+++ b/solution.py
@@ -280,7 +280,8 @@
     near = [ring_shift(part, True, by) for by in (1, -1, 2)]
     grad_b = scan_grad_b(x, grad, c, steps_t, a_log)
     near = jnp.concatenate([part] + after(near, grad_b))
-    far = [ring_shift(near, False, by) for by in (1, -1)]
+    following = ring_shift(near, False, -1)
+    far = [ring_shift(near, False, 1), following]
     other_b = swap_cores(grad_b)
     both_b = jnp.concatenate([grad_b, other_b])
 
@@ -296,7 +297,8 @@
     both_hidden = jnp.concatenate([kept, swap_cores(sent)])
 
     half = block // 2
-    last = jnp.concatenate([ring_shift(far[0][:half], False, 1), ring_shift(far[1][half:], False, -1)])
+    upper = ring_shift(far[1][half:], False, -1)
+    last = jnp.concatenate([ring_shift(far[0][:half], False, 1), upper])
 
     def columns(i):
         return both_hidden[:, i * block : (i + 1) * block]

time: 97.9 us -> 97.9 us (level)
  no operation moved by 1% of the time
where the time goes in v2:
time: 97.9 us; the launch traced here: 97.7 us
  starting transfers between devices  33.8 us (35%)
  waiting for transfers between devices  29 us (30%)
  Pallas kernels  22.4 us (23%)
  matrix products  7.16 us (7%)
  local copies, waits for them, and re-layouts  2.3 us (2%)
  other arithmetic  2 us (2%)
  between operations  1.02 us (1%)
    ppermute x13, waiting for transfers between devices, ring_shift(): return lax.ppermute(shard, ('x', 'y', 'core'), pairs)  28.3 us
    ppermute x13, starting transfers between devices, ring_shift(): return lax.ppermute(shard, ('x', 'y', 'core'), pairs)  18.4 us
    ppermute x6, starting transfers between devices, swap_cores(): return lax.ppermute(shard, 'core', [(0, 1), (1, 0)])  11.6 us
    pallas_call x1, Pallas kernels, scan_grad_b(): pl.pallas_call(grad_b_kernel, grid=(GROUPS,), in_specs=[BY_HEADS, BY_HEAD...  10 us
    pallas_call x2, Pallas kernels, scan_step_grad(): pl.pallas_call(functools.partial(step_grad_kernel, first), grid=(count,),...  9.4 us
    ppermute x3, starting transfers between devices, to_previous_section(): lax.ppermute(shard, 'section', [(s, s - 1) for s in range(1, lax.axis_siz...  3.88 us
    dot_general x4, matrix products, outer_dot(): lax.dot_general(a, b, (((0,), (0,)), ((), ())), preferred_element_type=F32)  2.57 us
    dot_general x4, matrix products, rows_dot(): return jnp.dot(a, b, preferred_element_type=F32)  2.36 us
  transfers between devices with their start and end apart: 22, of which 8 were waited for; matrix products, arithmetic and copies ran while one was open for 9% of the time, Pallas kernels for 23%

profile of v2, /device:TPU:1, one launch (start us, length us, event | category | flops | bytes accessed | tf_op | source)
XLA Modules:
  0.0 97.7 jit_solution(6682037736582601759)
XLA Ops:
  0.6 3.8 %collective-permute-start.4 = (bf16[256,768]{1,0:T(8,128)(2,1)}, bf16[256,768]{1,0:T(8,128)(2,1)S(1)}, u32[]{:S(2)}, u32[]{:S(2)}) collective-permute-start(bf16[256,768]{1,0:T(8,128)(2,1)} %bitcast.38), channel_id=1, source_target_pairs={{0,128},{8,40},{16,144},{24,56},{32,160},{40,8},{48,176},{56,24},{... | collective-permute-start | bytes 1179656 | tf_op jit(solution)/shard_map/ppermute | solution.py:38
  4.5 0.8 collective-permute-start.3
  5.2 0.7 collective-permute-start.2
  6.0 1.6 %copy-done.2 = bf16[1,128,8192]{2,1,0:T(8,128)(2,1)S(1)} copy-done((bf16[1,128,8192]{2,1,0:T(8,128)(2,1)S(1)}, bf16[1,128,8192]{2,1,0:T(8,128)(2,1)}, u32[]{:S(2)}) %copy-start.2) | copy-done | bytes 2097176
  7.6 0.8 split_columns.1
  8.4 1.4 %collective-permute-start = (bf16[128,4096]{1,0:T(8,128)(2,1)S(1)}, bf16[128,4096]{1,0:T(8,128)(2,1)S(1)}, u32[]{:S(2)}, u32[]{:S(2)}) collective-permute-start(bf16[128,4096]{1,0:T(8,128)(2,1)S(1)} %get-tuple-element.24), channel_id=1, source_target_pairs={{0,8},{8,0},{1,9},{9,1},{2,10},{10,2},{3,11},{11,3},{4,12},{12,4},... | collective-permute-start | bytes 3145736 | tf_op jit(solution)/shard_map/ppermute | solution.py:42
  9.9 10.0 %scan_grad_b.1 = bf16[128,768]{1,0:T(8,128)(2,1)} custom-call(bf16[128,12288]{1,0:T(8,128)(2,1)} %bitcast.24, bf16[128,12288]{1,0:T(8,128)(2,1)} %bitcast.27, bf16[128,768]{1,0:T(8,128)(2,1)} %bitcast.31, f32[192,128]{1,0:T(8,128)} %bitcast.34, f32[1,192]{1,0:T(1,128)} %alog_ref.5), custom_call_target="tpu_custom_call" | custom-call | bytes 1024 | tf_op jit(solution)/shard_map/scan_grad_b/pallas_call | solution.py:226
  20.0 2.1 %collective-permute-start.6 = (bf16[1024,768]{1,0:T(8,128)(2,1)S(1)}, bf16[1024,768]{1,0:T(8,128)(2,1)S(1)}, u32[]{:S(2)}, u32[]{:S(2)}) collective-permute-start(bf16[1024,768]{1,0:T(8,128)(2,1)S(1)} %pad_maximum_fusion), channel_id=1, source_target_pairs={{0,48},{8,200},{16,0},{24,216},{32,16},{40,232},{48,32},{56,248},{... | collective-permute-start | bytes 4718600 | tf_op jit(solution)/shard_map/ppermute | solution.py:38
  22.9 1.3 %collective-permute-start.7 = (bf16[256,1024]{1,0:T(8,128)(2,1)S(1)}, bf16[256,1024]{1,0:T(8,128)(2,1)S(1)}, u32[]{:S(2)}, u32[]{:S(2)}) collective-permute-start(bf16[256,1024]{1,0:T(8,128)(2,1)S(1)} %convolution_convert_fusion.1), channel_id=1, source_target_pairs={{1,0},{2,1},{3,2},{4,3},{5,4},{6,5},{7,6},{9,8},{10,9},{11,10},{12... | collective-permute-start | bytes 1572872 | tf_op jit(solution)/shard_map/ppermute | solution.py:46
  24.6 15.0 %collective-permute-done.6 = bf16[1024,768]{1,0:T(8,128)(2,1)S(1)} collective-permute-done((bf16[1024,768]{1,0:T(8,128)(2,1)S(1)}, bf16[1024,768]{1,0:T(8,128)(2,1)S(1)}, u32[]{:S(2)}, u32[]{:S(2)}) %collective-permute-start.6) | collective-permute-done | bytes 1572896 | tf_op jit(solution)/shard_map/ppermute | solution.py:38
  39.7 3.4 %collective-permute-start.10 = (bf16[512,768]{1,0:T(8,128)(2,1)S(1)}, bf16[512,768]{1,0:T(8,128)(2,1)S(1)}, u32[]{:S(2)}, u32[]{:S(2)}) collective-permute-start(bf16[512,768]{1,0:T(8,128)(2,1)S(1)} %slice.93), channel_id=1, source_target_pairs={{0,48},{8,200},{16,0},{24,216},{32,16},{40,232},{48,32},{56,248},{... | collective-permute-start | bytes 2359304 | tf_op jit(solution)/shard_map/ppermute | solution.py:38
  43.2 1.0 %fusion.4 = bf16[256,2048]{1,0:T(8,128)(2,1)S(1)} fusion(bf16[1024,768]{1,0:T(8,128)(2,1)S(1)} %collective-permute-done.6, bf16[1024,768]{1,0:T(8,128)(2,1)S(1)} %collective-permute-done.5, bf16[128,768]{1,0:T(8,128)(2,1)S(1)} %collective-permute-done.1, bf16[128,768]{1,0:T(8,128)(2,1)S(1)} %copy-done.6), kind=kOutput, calls=%fused_computation.5 | convolution fusion | flops 812908544 | bytes 4587520 | tf_op jit(solution)/shard_map/dot_general | solution.py:267
  44.3 1.3 %collective-permute-start.15 = (bf16[256,2048]{1,0:T(8,128)(2,1)S(1)}, bf16[256,2048]{1,0:T(8,128)(2,1)S(1)}, u32[]{:S(2)}, u32[]{:S(2)}) collective-permute-start(bf16[256,2048]{1,0:T(8,128)(2,1)S(1)} %fusion.4), channel_id=1, source_target_pairs={{1,0},{2,1},{3,2},{4,3},{5,4},{6,5},{7,6},{9,8},{10,9},{11,10},{12... | collective-permute-start | bytes 3145736 | tf_op jit(solution)/shard_map/ppermute | solution.py:46
  45.6 2.7 %collective-permute-start.8 = (bf16[256,1792]{1,0:T(8,128)(2,1)S(1)}, bf16[256,1792]{1,0:T(8,128)(2,1)S(1)}, u32[]{:S(2)}, u32[]{:S(2)}) collective-permute-start(bf16[256,1792]{1,0:T(8,128)(2,1)S(1)} %get-tuple-element.29), channel_id=1, source_target_pairs={{0,48},{8,200},{16,0},{24,216},{32,16},{40,232},{48,32},{56,248},{... | collective-permute-start | bytes 2752520 | tf_op jit(solution)/shard_map/ppermute | solution.py:38
  49.5 6.1 %collective-permute-done.9 = bf16[512,768]{1,0:T(8,128)(2,1)S(1)} collective-permute-done((bf16[512,768]{1,0:T(8,128)(2,1)S(1)}, bf16[512,768]{1,0:T(8,128)(2,1)S(1)}, u32[]{:S(2)}, u32[]{:S(2)}) %collective-permute-start.9) | collective-permute-done | bytes 786464 | tf_op jit(solution)/shard_map/ppermute | solution.py:38
  56.3 0.6 fusion.8
  57.0 3.2 %collective-permute-start.11 = (f32[128,768]{1,0:T(8,128)S(1)}, f32[128,768]{1,0:T(8,128)S(1)}, u32[]{:S(2)}, u32[]{:S(2)}) collective-permute-start(f32[128,768]{1,0:T(8,128)S(1)} %slice.95), channel_id=1, source_target_pairs={{0,8},{8,0},{1,9},{9,1},{2,10},{10,2},{3,11},{11,3},{4,12},{12,4},... | collective-permute-start | bytes 1179656 | tf_op jit(solution)/shard_map/ppermute | solution.py:42
  61.0 0.8 collective-permute-done.8
  61.9 3.5 %collective-permute-done.12 = bf16[256,1792]{1,0:T(8,128)(2,1)S(1)} collective-permute-done((bf16[256,1792]{1,0:T(8,128)(2,1)S(1)}, bf16[256,1792]{1,0:T(8,128)(2,1)S(1)}, u32[]{:S(2)}, u32[]{:S(2)}) %collective-permute-start.12) | collective-permute-done | bytes 917536 | tf_op jit(solution)/shard_map/ppermute | solution.py:38
  65.5 4.7 %scan_step_grad.2 = f32[96,128]{1,0:T(8,128)S(1)} custom-call(bf16[128,12288]{1,0:T(8,128)(2,1)S(1)} %bitcast.25, bf16[128,12288]{1,0:T(8,128)(2,1)S(1)} %bitcast.28, bf16[128,768]{1,0:T(8,128)(2,1)S(1)} %bitcast.32, bf16[128,768]{1,0:T(8,128)(2,1)S(1)} %fusion.21.b_ref, f32[192,128]{1,0:T(8,128)S(1)} %bitcast.35, f32[1,192]{1,0:T(1,128)S(1)} %copy-done.5), custom_call_target="tpu_custom_call" | custom-call | bytes 1024 | tf_op jit(solution)/shard_map/scan_step_grad/pallas_call | solution.py:242
  70.3 3.2 %collective-permute-start.16 = (bf16[128,2048]{1,0:T(8,128)(2,1)S(1)}, bf16[128,2048]{1,0:T(8,128)(2,1)S(1)}, u32[]{:S(2)}, u32[]{:S(2)}) collective-permute-start(bf16[128,2048]{1,0:T(8,128)(2,1)S(1)} %slice.83), channel_id=1, source_target_pairs={{0,8},{8,0},{1,9},{9,1},{2,10},{10,2},{3,11},{11,3},{4,12},{12,4},... | collective-permute-start | bytes 1572872 | tf_op jit(solution)/shard_map/ppermute | solution.py:42
  74.2 1.3 %collective-permute-start.20 = (bf16[256,1024]{1,0:T(8,128)(2,1)S(1)}, bf16[256,1024]{1,0:T(8,128)(2,1)S(1)}, u32[]{:S(2)}, u32[]{:S(2)}) collective-permute-start(bf16[256,1024]{1,0:T(8,128)(2,1)S(1)} %convolution_convert_fusion), channel_id=1, source_target_pairs={{1,0},{2,1},{3,2},{4,3},{5,4},{6,5},{7,6},{9,8},{10,9},{11,10},{12... | collective-permute-start | bytes 1572872 | tf_op jit(solution)/shard_map/ppermute | solution.py:46
  76.7 2.7 %collective-permute-done.13 = bf16[256,1792]{1,0:T(8,128)(2,1)S(1)} collective-permute-done((bf16[256,1792]{1,0:T(8,128)(2,1)S(1)}, bf16[256,1792]{1,0:T(8,128)(2,1)S(1)}, u32[]{:S(2)}, u32[]{:S(2)}) %collective-permute-start.13) | collective-permute-done | bytes 917536 | tf_op jit(solution)/shard_map/ppermute | solution.py:38
  79.4 0.7 fusion.35
  80.3 2.1 %collective-permute-start.19 = (bf16[256,768]{1,0:T(8,128)(2,1)S(1)}, bf16[256,768]{1,0:T(8,128)(2,1)S(1)}, u32[]{:S(2)}, u32[]{:S(2)}) collective-permute-start(bf16[256,768]{1,0:T(8,128)(2,1)S(1)} %get-tuple-element.46), channel_id=1, source_target_pairs={{0,128},{8,40},{16,144},{24,56},{32,160},{40,8},{48,176},{56,24},{... | collective-permute-start | bytes 1179656 | tf_op jit(solution)/shard_map/ppermute | solution.py:38
  82.4 1.0 %collective-permute-start.18 = (bf16[256,768]{1,0:T(8,128)(2,1)S(1)}, bf16[256,768]{1,0:T(8,128)(2,1)S(1)}, u32[]{:S(2)}, u32[]{:S(2)}) collective-permute-start(bf16[256,768]{1,0:T(8,128)(2,1)S(1)} %get-tuple-element.47), channel_id=1, source_target_pairs={{0,64},{8,24},{16,80},{24,40},{32,96},{40,56},{48,112},{56,8},{64,... | collective-permute-start | bytes 1179656 | tf_op jit(solution)/shard_map/ppermute | solution.py:38
  83.4 1.7 %collective-permute-start.17 = (bf16[256,768]{1,0:T(8,128)(2,1)S(1)}, bf16[256,768]{1,0:T(8,128)(2,1)S(1)}, u32[]{:S(2)}, u32[]{:S(2)}) collective-permute-start(bf16[256,768]{1,0:T(8,128)(2,1)S(1)} %get-tuple-element.48), channel_id=1, source_target_pairs={{0,192},{8,56},{16,208},{24,8},{32,224},{40,24},{48,240},{56,40},{... | collective-permute-start | bytes 1179656 | tf_op jit(solution)/shard_map/ppermute | solution.py:38
  85.0 4.7 %scan_step_grad.3 = f32[96,128]{1,0:T(8,128)S(1)} custom-call(bf16[128,12288]{1,0:T(8,128)(2,1)S(1)} %bitcast.26, bf16[128,12288]{1,0:T(8,128)(2,1)S(1)} %bitcast.29, bf16[128,768]{1,0:T(8,128)(2,1)S(1)} %bitcast.33, bf16[128,768]{1,0:T(8,128)(2,1)S(1)} %fusion.21.b_ref, f32[192,128]{1,0:T(8,128)S(1)} %bitcast.36, f32[1,192]{1,0:T(1,128)S(1)} %copy-done.5), custom_call_target="tpu_custom_call" | custom-call | bytes 1024 | tf_op jit(solution)/shard_map/scan_step_grad/pallas_call | solution.py:242
  89.9 3.5 %collective-permute-start.21 = (bf16[128,1024]{1,0:T(8,128)(2,1)S(1)}, bf16[128,1024]{1,0:T(8,128)(2,1)S(1)}, u32[]{:S(2)}, u32[]{:S(2)}) collective-permute-start(bf16[128,1024]{1,0:T(8,128)(2,1)S(1)} %slice.87), channel_id=1, source_target_pairs={{0,8},{8,0},{1,9},{9,1},{2,10},{10,2},{3,11},{11,3},{4,12},{12,4},... | collective-permute-start | bytes 786440 | tf_op jit(solution)/shard_map/ppermute | solution.py:42
  93.4 0.6 fusion.26
  94.6 2.1 %join_columns.1 = bf16[128,8192]{1,0:T(8,128)(2,1)} custom-call(s32[3]{0:T(128)S(1)} %pad_add_fusion.where_ref, bf16[256,1024]{1,0:T(8,128)(2,1)S(1)} %collective-permute-done.7.refs_0_, bf16[128,1024]{1,0:T(8,128)(2,1)S(1)} %collective-permute-done.14.refs_1_, bf16[256,2048]{1,0:T(8,128)(2,1)S(1)} %collective-permute-done.15.refs_2_, ...), custom_call_target="tpu_custom_call" | custom-call | bytes 1024 | tf_op jit(solution)/shard_map/join_columns/pallas_call | solution.py:98
  96.7 0.9 fusion.20
  (62 shorter events, 6.9 us)
Async XLA Ops:
  0.6 19.3 %collective-permute-start.4 = (bf16[256,768]{1,0:T(8,128)(2,1)}, bf16[256,768]{1,0:T(8,128)(2,1)S(1)}, u32[]{:S(2)}, u32[]{:S(2)}) collective-permute-start(bf16[256,768]{1,0:T(8,128)(2,1)} %bitcast.38), channel_id=1, source_target_pairs={{0,128},{8,40},{16,144},{24,56},{32,160},{40,8},{48,176},{56,24},{... | collective-permute-start | bytes 1179656 | tf_op jit(solution)/shard_map/ppermute | solution.py:38
  4.5 15.5 %collective-permute-start.3 = (bf16[256,768]{1,0:T(8,128)(2,1)}, bf16[256,768]{1,0:T(8,128)(2,1)S(1)}, u32[]{:S(2)}, u32[]{:S(2)}) collective-permute-start(bf16[256,768]{1,0:T(8,128)(2,1)} %bitcast.39), channel_id=1, source_target_pairs={{0,192},{8,56},{16,208},{24,8},{32,224},{40,24},{48,240},{56,40},{... | collective-permute-start | bytes 1179656 | tf_op jit(solution)/shard_map/ppermute | solution.py:38
  5.2 14.7 %collective-permute-start.2 = (bf16[256,768]{1,0:T(8,128)(2,1)}, bf16[256,768]{1,0:T(8,128)(2,1)S(1)}, u32[]{:S(2)}, u32[]{:S(2)}) collective-permute-start(bf16[256,768]{1,0:T(8,128)(2,1)} %bitcast.40), channel_id=1, source_target_pairs={{0,64},{8,24},{16,80},{24,40},{32,96},{40,56},{48,112},{56,8},{64,... | collective-permute-start | bytes 1179656 | tf_op jit(solution)/shard_map/ppermute | solution.py:38
  6.0 1.6 %copy-start.2 = (bf16[1,128,8192]{2,1,0:T(8,128)(2,1)S(1)}, bf16[1,128,8192]{2,1,0:T(8,128)(2,1)}, u32[]{:S(2)}) copy-start(bf16[1,128,8192]{2,1,0:T(8,128)(2,1)} %param.7) | copy-start | bytes 6291460
  8.4 15.8 %collective-permute-start = (bf16[128,4096]{1,0:T(8,128)(2,1)S(1)}, bf16[128,4096]{1,0:T(8,128)(2,1)S(1)}, u32[]{:S(2)}, u32[]{:S(2)}) collective-permute-start(bf16[128,4096]{1,0:T(8,128)(2,1)S(1)} %get-tuple-element.24), channel_id=1, source_target_pairs={{0,8},{8,0},{1,9},{9,1},{2,10},{10,2},{3,11},{11,3},{4,12},{12,4},... | collective-permute-start | bytes 3145736 | tf_op jit(solution)/shard_map/ppermute | solution.py:42
  9.9 10.1 %copy-start.7 = (bf16[1,256,768]{2,1,0:T(8,128)(2,1)S(1)}, bf16[1,256,768]{2,1,0:T(8,128)(2,1)}, u32[]{:S(2)}) copy-start(bf16[1,256,768]{2,1,0:T(8,128)(2,1)} %param.8) | copy-start | bytes 1179652
  19.9 2.4 %copy-start.6 = (bf16[128,768]{1,0:T(8,128)(2,1)S(1)}, bf16[128,768]{1,0:T(8,128)(2,1)}, u32[]{:S(2)}) copy-start(bf16[128,768]{1,0:T(8,128)(2,1)} %scan_grad_b.1) | copy-start | bytes 589828
  19.9 2.4 %collective-permute-start.1 = (bf16[128,768]{1,0:T(8,128)(2,1)}, bf16[128,768]{1,0:T(8,128)(2,1)S(1)}, u32[]{:S(2)}, u32[]{:S(2)}) collective-permute-start(bf16[128,768]{1,0:T(8,128)(2,1)} %scan_grad_b.1), channel_id=1, source_target_pairs={{0,8},{8,0},{1,9},{9,1},{2,10},{10,2},{3,11},{11,3},{4,12},{12,4},... | collective-permute-start | bytes 589832 | tf_op jit(solution)/shard_map/ppermute | solution.py:42
  20.0 19.6 %collective-permute-start.6 = (bf16[1024,768]{1,0:T(8,128)(2,1)S(1)}, bf16[1024,768]{1,0:T(8,128)(2,1)S(1)}, u32[]{:S(2)}, u32[]{:S(2)}) collective-permute-start(bf16[1024,768]{1,0:T(8,128)(2,1)S(1)} %pad_maximum_fusion), channel_id=1, source_target_pairs={{0,48},{8,200},{16,0},{24,216},{32,16},{40,232},{48,32},{56,248},{... | collective-permute-start | bytes 4718600 | tf_op jit(solution)/shard_map/ppermute | solution.py:38
  22.2 20.9 %collective-permute-start.5 = (bf16[1024,768]{1,0:T(8,128)(2,1)S(1)}, bf16[1024,768]{1,0:T(8,128)(2,1)S(1)}, u32[]{:S(2)}, u32[]{:S(2)}) collective-permute-start(bf16[1024,768]{1,0:T(8,128)(2,1)S(1)} %pad_maximum_fusion), channel_id=1, source_target_pairs={{0,16},{8,72},{16,32},{24,88},{32,48},{40,104},{48,0},{56,120},{64... | collective-permute-start | bytes 4718600 | tf_op jit(solution)/shard_map/ppermute | solution.py:38
  22.9 21.4 %collective-permute-start.7 = (bf16[256,1024]{1,0:T(8,128)(2,1)S(1)}, bf16[256,1024]{1,0:T(8,128)(2,1)S(1)}, u32[]{:S(2)}, u32[]{:S(2)}) collective-permute-start(bf16[256,1024]{1,0:T(8,128)(2,1)S(1)} %convolution_convert_fusion.1), channel_id=1, source_target_pairs={{1,0},{2,1},{3,2},{4,3},{5,4},{6,5},{7,6},{9,8},{10,9},{11,10},{12... | collective-permute-start | bytes 1572872 | tf_op jit(solution)/shard_map/ppermute | solution.py:46
  39.7 15.9 %collective-permute-start.10 = (bf16[512,768]{1,0:T(8,128)(2,1)S(1)}, bf16[512,768]{1,0:T(8,128)(2,1)S(1)}, u32[]{:S(2)}, u32[]{:S(2)}) collective-permute-start(bf16[512,768]{1,0:T(8,128)(2,1)S(1)} %slice.93), channel_id=1, source_target_pairs={{0,48},{8,200},{16,0},{24,216},{32,16},{40,232},{48,32},{56,248},{... | collective-permute-start | bytes 2359304 | tf_op jit(solution)/shard_map/ppermute | solution.py:38
  43.1 12.4 %collective-permute-start.9 = (bf16[512,768]{1,0:T(8,128)(2,1)S(1)}, bf16[512,768]{1,0:T(8,128)(2,1)S(1)}, u32[]{:S(2)}, u32[]{:S(2)}) collective-permute-start(bf16[512,768]{1,0:T(8,128)(2,1)S(1)} %slice.92), channel_id=1, source_target_pairs={{0,16},{8,72},{16,32},{24,88},{32,48},{40,104},{48,0},{56,120},{64... | collective-permute-start | bytes 2359304 | tf_op jit(solution)/shard_map/ppermute | solution.py:38
  44.3 26.0 %collective-permute-start.15 = (bf16[256,2048]{1,0:T(8,128)(2,1)S(1)}, bf16[256,2048]{1,0:T(8,128)(2,1)S(1)}, u32[]{:S(2)}, u32[]{:S(2)}) collective-permute-start(bf16[256,2048]{1,0:T(8,128)(2,1)S(1)} %fusion.4), channel_id=1, source_target_pairs={{1,0},{2,1},{3,2},{4,3},{5,4},{6,5},{7,6},{9,8},{10,9},{11,10},{12... | collective-permute-start | bytes 3145736 | tf_op jit(solution)/shard_map/ppermute | solution.py:46
  45.6 16.3 %collective-permute-start.8 = (bf16[256,1792]{1,0:T(8,128)(2,1)S(1)}, bf16[256,1792]{1,0:T(8,128)(2,1)S(1)}, u32[]{:S(2)}, u32[]{:S(2)}) collective-permute-start(bf16[256,1792]{1,0:T(8,128)(2,1)S(1)} %get-tuple-element.29), channel_id=1, source_target_pairs={{0,48},{8,200},{16,0},{24,216},{32,16},{40,232},{48,32},{56,248},{... | collective-permute-start | bytes 2752520 | tf_op jit(solution)/shard_map/ppermute | solution.py:38
  48.3 17.1 %collective-permute-start.12 = (bf16[256,1792]{1,0:T(8,128)(2,1)S(1)}, bf16[256,1792]{1,0:T(8,128)(2,1)S(1)}, u32[]{:S(2)}, u32[]{:S(2)}) collective-permute-start(bf16[256,1792]{1,0:T(8,128)(2,1)S(1)} %get-tuple-element.31), channel_id=1, source_target_pairs={{0,16},{8,72},{16,32},{24,88},{32,48},{40,104},{48,0},{56,120},{64... | collective-permute-start | bytes 2752520 | tf_op jit(solution)/shard_map/ppermute | solution.py:38
  56.3 9.2 %copy-start.3 = (bf16[1,128,768]{2,1,0:T(8,128)(2,1)S(1)}, bf16[1,128,768]{2,1,0:T(8,128)(2,1)}, u32[]{:S(2)}) copy-start(bf16[1,128,768]{2,1,0:T(8,128)(2,1)} %param.10) | copy-start | bytes 589828
  56.3 9.2 %copy-start.4 = (f32[1,128,192]{1,2,0:T(8,128)S(1)}, f32[1,128,192]{1,2,0:T(8,128)}, u32[]{:S(2)}) copy-start(f32[1,128,192]{1,2,0:T(8,128)} %param.11) | copy-start | bytes 294916
  57.0 8.5 %copy-start.1 = (bf16[1,128,12288]{2,1,0:T(8,128)(2,1)S(1)}, bf16[1,128,12288]{2,1,0:T(8,128)(2,1)}, u32[]{:S(2)}) copy-start(bf16[1,128,12288]{2,1,0:T(8,128)(2,1)} %param.13) | copy-start | bytes 9437188
  57.0 8.5 %copy-start = (bf16[1,128,12288]{2,1,0:T(8,128)(2,1)S(1)}, bf16[1,128,12288]{2,1,0:T(8,128)(2,1)}, u32[]{:S(2)}) copy-start(bf16[1,128,12288]{2,1,0:T(8,128)(2,1)} %param.9) | copy-start | bytes 9437188
  57.0 8.5 %copy-start.5 = (f32[1,192]{1,0:T(1,128)S(1)}, f32[1,192]{1,0:T(1,128)}, u32[]{:S(2)}) copy-start(f32[1,192]{1,0:T(1,128)} %alog_ref.5) | copy-start | bytes 2308
  57.0 8.4 %collective-permute-start.11 = (f32[128,768]{1,0:T(8,128)S(1)}, f32[128,768]{1,0:T(8,128)S(1)}, u32[]{:S(2)}, u32[]{:S(2)}) collective-permute-start(f32[128,768]{1,0:T(8,128)S(1)} %slice.95), channel_id=1, source_target_pairs={{0,8},{8,0},{1,9},{9,1},{2,10},{10,2},{3,11},{11,3},{4,12},{12,4},... | collective-permute-start | bytes 1179656 | tf_op jit(solution)/shard_map/ppermute | solution.py:42
  60.9 19.2 %collective-permute-start.14 = (bf16[128,1024]{1,0:T(8,128)(2,1)S(1)}, bf16[128,1024]{1,0:T(8,128)(2,1)S(1)}, u32[]{:S(2)}, u32[]{:S(2)}) collective-permute-start(bf16[128,1024]{1,0:T(8,128)(2,1)S(1)} %slice.82), channel_id=1, source_target_pairs={{0,8},{8,0},{1,9},{9,1},{2,10},{10,2},{3,11},{11,3},{4,12},{12,4},... | collective-permute-start | bytes 786440 | tf_op jit(solution)/shard_map/ppermute | solution.py:42
  65.4 14.0 %collective-permute-start.13 = (bf16[256,1792]{1,0:T(8,128)(2,1)S(1)}, bf16[256,1792]{1,0:T(8,128)(2,1)S(1)}, u32[]{:S(2)}, u32[]{:S(2)}) collective-permute-start(bf16[256,1792]{1,0:T(8,128)(2,1)S(1)} %get-tuple-element.33), channel_id=1, source_target_pairs={{0,32},{8,136},{16,48},{24,152},{32,0},{40,168},{48,16},{56,184},{... | collective-permute-start | bytes 2752520 | tf_op jit(solution)/shard_map/ppermute | solution.py:38
  70.3 9.9 %collective-permute-start.16 = (bf16[128,2048]{1,0:T(8,128)(2,1)S(1)}, bf16[128,2048]{1,0:T(8,128)(2,1)S(1)}, u32[]{:S(2)}, u32[]{:S(2)}) collective-permute-start(bf16[128,2048]{1,0:T(8,128)(2,1)S(1)} %slice.83), channel_id=1, source_target_pairs={{0,8},{8,0},{1,9},{9,1},{2,10},{10,2},{3,11},{11,3},{4,12},{12,4},... | collective-permute-start | bytes 1572872 | tf_op jit(solution)/shard_map/ppermute | solution.py:42
  74.2 15.7 %collective-permute-start.20 = (bf16[256,1024]{1,0:T(8,128)(2,1)S(1)}, bf16[256,1024]{1,0:T(8,128)(2,1)S(1)}, u32[]{:S(2)}, u32[]{:S(2)}) collective-permute-start(bf16[256,1024]{1,0:T(8,128)(2,1)S(1)} %convolution_convert_fusion), channel_id=1, source_target_pairs={{1,0},{2,1},{3,2},{4,3},{5,4},{6,5},{7,6},{9,8},{10,9},{11,10},{12... | collective-permute-start | bytes 1572872 | tf_op jit(solution)/shard_map/ppermute | solution.py:46
  80.3 16.4 %collective-permute-start.19 = (bf16[256,768]{1,0:T(8,128)(2,1)S(1)}, bf16[256,768]{1,0:T(8,128)(2,1)S(1)}, u32[]{:S(2)}, u32[]{:S(2)}) collective-permute-start(bf16[256,768]{1,0:T(8,128)(2,1)S(1)} %get-tuple-element.46), channel_id=1, source_target_pairs={{0,128},{8,40},{16,144},{24,56},{32,160},{40,8},{48,176},{56,24},{... | collective-permute-start | bytes 1179656 | tf_op jit(solution)/shard_map/ppermute | solution.py:38
  82.4 14.3 %collective-permute-start.18 = (bf16[256,768]{1,0:T(8,128)(2,1)S(1)}, bf16[256,768]{1,0:T(8,128)(2,1)S(1)}, u32[]{:S(2)}, u32[]{:S(2)}) collective-permute-start(bf16[256,768]{1,0:T(8,128)(2,1)S(1)} %get-tuple-element.47), channel_id=1, source_target_pairs={{0,64},{8,24},{16,80},{24,40},{32,96},{40,56},{48,112},{56,8},{64,... | collective-permute-start | bytes 1179656 | tf_op jit(solution)/shard_map/ppermute | solution.py:38
  83.4 13.3 %collective-permute-start.17 = (bf16[256,768]{1,0:T(8,128)(2,1)S(1)}, bf16[256,768]{1,0:T(8,128)(2,1)S(1)}, u32[]{:S(2)}, u32[]{:S(2)}) collective-permute-start(bf16[256,768]{1,0:T(8,128)(2,1)S(1)} %get-tuple-element.48), channel_id=1, source_target_pairs={{0,192},{8,56},{16,208},{24,8},{32,224},{40,24},{48,240},{56,40},{... | collective-permute-start | bytes 1179656 | tf_op jit(solution)/shard_map/ppermute | solution.py:38
  89.9 4.7 %collective-permute-start.21 = (bf16[128,1024]{1,0:T(8,128)(2,1)S(1)}, bf16[128,1024]{1,0:T(8,128)(2,1)S(1)}, u32[]{:S(2)}, u32[]{:S(2)}) collective-permute-start(bf16[128,1024]{1,0:T(8,128)(2,1)S(1)} %slice.87), channel_id=1, source_target_pairs={{0,8},{8,0},{1,9},{9,1},{2,10},{10,2},{3,11},{11,3},{4,12},{12,4},... | collective-permute-start | bytes 786440 | tf_op jit(solution)/shard_map/ppermute | solution.py:42
